TPU v7x, 128 devices: a whole 4x4x4 slice. The times are simulated.
128 devices in a mesh: series: 4 (over x), tm: 32 (over z, y, core).
Axes of the slice: x: 4, y: 4, z: 4, core: 2. Of those that a mesh axis runs over, the one named last changes fastest.
Arguments:
- raw_values: float32 [4, 4096], P('series', 'tm'), may hold values from -6 to 6
- hours: int32 [4, 4096], P('series', 'tm'), may hold values from 0 to 23
- doc_lengths: int32 [4, 7], P('series'), may hold values from 16 to 4000, as said below
- doc_scale: float32 [4, 7], P('series'), may hold values from 0.5 to 2
- dataset_ids: int32 [4, 7, 1], P('series'), may hold values from 0 to 7
- lag_offsets: int32 [84], replicated, may hold values from 1 to 384, as said below
- w_lag: bfloat16 [87, 144], replicated, may hold values from -0.625 to 0.625
- w_qkv: bfloat16 [2, 144, 432], replicated, may hold values from -0.5 to 0.5
- w_out: bfloat16 [2, 144, 144], replicated, may hold values from -1.5 to 1.5
- w_gate_up: bfloat16 [2, 144, 768], replicated, may hold values from -0.5 to 0.5
- w_down: bfloat16 [2, 384, 144], replicated, may hold values from -0.3125 to 0.3125
- gains: float32 [2, 2, 144], replicated, may hold values from 0.5 to 1.5
- cotangent: float32 [4, 4096, 144], P('series', 'tm'), may hold values from -6 to 6
Outputs:
- activations: float32 [4, 4096, 144], P('series', 'tm')
- raw_grad: float32 [4, 4096], P('series', 'tm')
- scale_mean: float32 [8], replicated
- w_lag_grad: float32 [87, 144], replicated
- w_qkv_grad: float32 [2, 144, 432], replicated
- w_out_grad: float32 [2, 144, 144], replicated
- w_gate_up_grad: float32 [2, 144, 768], replicated
- w_down_grad: float32 [2, 384, 144], replicated
- gains_grad: float32 [2, 2, 144], replicated
Inputs may be any that keep to these rules, and one draw needn't show every extreme that they name: `doc_lengths`: each row holds 3 short series, then one long series, then 3 short series; short ones have 32 // 2 to 32 steps; the row sums to 4096. `lag_offsets`: distinct and rising, the last equal to 384.
All inputs are finite; a program needn't handle non-finite values.
Results may differ from a plain program's by a relative error of at most 0.025.
Values may be sent and summed in bfloat16 or wider, within the bound.
No kernel may reach another device: no remote copies, remote signals or barrier semaphores. Data moves between devices by JAX's collectives and lax.ppermute only.
A program may use at most 192 MiB of HBM per device.

v0:
```python
import math

import jax
import jax.numpy as jnp
from jax import lax
from jax.sharding import PartitionSpec as P

D = 144
HEADS = 9
HEAD_DIM = 16
FF = 384
LAYERS = 2
HALO_BLOCKS = 3
DATASETS = 8
MAXLAG = 384


EPSILON = 1e-06
MASKED = -1e30


def shifted(block, axis, distance):
    devices = range(lax.axis_size(axis))
    route = [(i - distance, i) for i in devices if i - distance in devices]
    return lax.ppermute(block, axis, route)


def side_by_side(arrays, axis, dim, along):
    both = jnp.concatenate(arrays, axis=along)
    out, at, done = (lax.all_gather(both, axis, axis=dim, tiled=True), 0, [])
    for a in arrays:
        done.append(lax.slice_in_dim(out, at, at + a.shape[along], axis=along))
        at += a.shape[along]
    return tuple(done)


def doc_info(places, lengths, scales):
    ends = jnp.cumsum(lengths)
    after = places[:, None] >= ends[None, :]
    which = jnp.sum(after.astype(jnp.int32), axis=1)
    start = jnp.sum(jnp.where(after, lengths[None, :], 0), axis=1)
    labels = jnp.arange(lengths.shape[0], dtype=jnp.int32)
    picked = jnp.sum(
        jnp.where(which[:, None] == labels[None, :], scales[None, :], jnp.float32(0.0)), axis=1
    )
    return (which, start, picked)


def lag_features(extended, places, local_rows, lag_offsets, hours, start, own_scale):
    index = MAXLAG + local_rows[:, None] - lag_offsets[None, :]
    lagged = jnp.take(extended, index)
    valid = places[:, None] - lag_offsets[None, :] >= start[:, None]
    values = jnp.where(valid, lagged, jnp.float32(0.0)) / own_scale[:, None]
    angle = hours.astype(jnp.float32) * (2.0 * math.pi / 24.0)
    return jnp.concatenate(
        [values, jnp.sin(angle)[:, None], jnp.cos(angle)[:, None], jnp.log(own_scale)[:, None]],
        axis=1,
    )


def rope_turn(field, places, sign):
    rows = field.shape[0]
    shaped = field.reshape(rows, HEADS, HEAD_DIM)
    half = HEAD_DIM // 2
    freqs = 10000.0 ** (-jnp.arange(half, dtype=jnp.float32) / half)
    angle = places.astype(jnp.float32)[:, None] * freqs[None, :]
    cosine = jnp.cos(angle)[:, None, :]
    sine = sign * jnp.sin(angle)[:, None, :]
    first = shaped[..., :half]
    second = shaped[..., half:]
    turned = jnp.concatenate(
        [first * cosine - second * sine, second * cosine + first * sine], axis=-1
    )
    return turned.reshape(rows, HEADS * HEAD_DIM)


def normed(resid, gain):
    factor = lax.rsqrt(jnp.mean(resid * resid, axis=-1, keepdims=True) + EPSILON)
    return resid * factor * gain


def gated(gate_up):
    return jax.nn.silu(gate_up[:, :FF]) * gate_up[:, FF:]


def scores_of(queries, keys, allowed):
    raw = jnp.einsum(
        "thd,jhd->htj", queries, keys, preferred_element_type=jnp.float32
    ) * HEAD_DIM ** (-0.5)
    return jnp.where(allowed[None], raw, MASKED)


def body(
    raw_values,
    hours,
    doc_lengths,
    doc_scale,
    dataset_ids,
    lag_offsets,
    w_lag,
    w_qkv,
    w_out,
    w_gate_up,
    w_down,
    gains,
    cotangent,
):
    bf16 = jnp.bfloat16
    f32 = jnp.float32
    factor = HEAD_DIM ** (-0.5)
    rows = raw_values.shape[1]
    span = rows * lax.axis_size("tm")
    first = lax.axis_index("tm") * rows
    local_rows = jnp.arange(rows, dtype=jnp.int32)
    places = first + local_rows
    every_place = jnp.arange(span, dtype=jnp.int32)
    lengths = doc_lengths[0]
    scales = doc_scale[0]
    which, start, own_scale = doc_info(places, lengths, scales)
    every_which = doc_info(every_place, lengths, scales)[0]
    allowed = (every_which[None, :] == which[:, None]) & (every_place[None, :] <= places[:, None])
    blocks = [shifted(raw_values, "tm", step) for step in range(HALO_BLOCKS, 0, -1)]
    extended = jnp.concatenate(blocks + [raw_values], axis=1)[0]

    def features_of(source):
        return lag_features(source, places, local_rows, lag_offsets, hours[0], start, own_scale)

    feats_full, feature_back = jax.vjp(features_of, extended)
    feats = feats_full.astype(bf16)
    resid = jnp.dot(feats, w_lag, preferred_element_type=f32)
    kept = []
    for layer in range(LAYERS):
        resid_in = resid
        normal_a = normed(resid, gains[layer, 0]).astype(bf16)
        mixed = jnp.dot(normal_a, w_qkv[layer], preferred_element_type=f32)
        query = rope_turn(mixed[:, :D], places, 1.0).astype(bf16).reshape(rows, HEADS, HEAD_DIM)
        key_rows = (
            rope_turn(mixed[:, D : 2 * D], places, 1.0).astype(bf16).reshape(rows, HEADS, HEAD_DIM)
        )
        value_rows = mixed[:, 2 * D :].astype(bf16).reshape(rows, HEADS, HEAD_DIM)
        key_all, value_all = side_by_side((key_rows, value_rows), "tm", 0, 1)
        scores = scores_of(query, key_all, allowed)
        top = jnp.max(scores, axis=-1, keepdims=True)
        expo = jnp.exp(scores - top)
        total = jnp.sum(expo, axis=-1, keepdims=True)
        probs_low = (expo / total).astype(bf16)
        attended = (
            jnp.einsum("htj,jhd->thd", probs_low, value_all, preferred_element_type=f32)
            .astype(bf16)
            .reshape(rows, D)
        )
        resid = resid + jnp.dot(attended, w_out[layer], preferred_element_type=f32)
        resid_mid = resid
        normal_b = normed(resid, gains[layer, 1]).astype(bf16)
        gate_up = jnp.dot(normal_b, w_gate_up[layer], preferred_element_type=f32)
        hidden = gated(gate_up).astype(bf16)
        resid = resid + jnp.dot(hidden, w_down[layer], preferred_element_type=f32)
        kept.append(
            (
                resid_in,
                normal_a,
                query,
                key_rows,
                value_rows,
                key_all,
                value_all,
                top,
                total,
                attended,
                resid_mid,
                normal_b,
                gate_up,
                hidden,
            )
        )
    grad = cotangent[0]
    layer_terms = [None] * LAYERS
    for layer in range(LAYERS - 1, -1, -1):
        (
            resid_in,
            normal_a,
            query,
            key_rows,
            value_rows,
            key_all,
            value_all,
            top,
            total,
            attended,
            resid_mid,
            normal_b,
            gate_up,
            hidden,
        ) = kept[layer]
        d_out = grad.astype(bf16)
        g_down = jnp.dot(hidden.T, d_out, preferred_element_type=f32)
        d_hidden = jnp.dot(d_out, w_down[layer].T, preferred_element_type=f32)
        d_gate_up = jax.vjp(gated, gate_up)[1](d_hidden)[0].astype(bf16)
        g_gate_up = jnp.dot(normal_b.T, d_gate_up, preferred_element_type=f32)
        d_normal_b = jnp.dot(d_gate_up, w_gate_up[layer].T, preferred_element_type=f32)
        d_mid, d_gain_b = jax.vjp(normed, resid_mid, gains[layer, 1])[1](d_normal_b)
        grad = grad + d_mid
        d_branch = grad.astype(bf16)
        g_out = jnp.dot(attended.T, d_branch, preferred_element_type=f32)
        d_att = (
            jnp.dot(d_branch, w_out[layer].T, preferred_element_type=f32)
            .astype(bf16)
            .reshape(rows, HEADS, HEAD_DIM)
        )
        scores = scores_of(query, key_all, allowed)
        probs = jnp.exp(scores - top) / total
        probs_low = probs.astype(bf16)
        d_probs = jnp.einsum("thd,jhd->htj", d_att, value_all, preferred_element_type=f32)
        delta = jnp.sum(d_probs * probs, axis=-1, keepdims=True)
        d_scores = (probs * (d_probs - delta)).astype(bf16)
        d_query = jnp.einsum("htj,jhd->thd", d_scores, key_all, preferred_element_type=f32) * factor
        query_all, d_att_all = side_by_side((query, d_att), "tm", 0, 1)
        top_all, total_all, delta_all = side_by_side((top, total, delta), "tm", 1, 0)
        reverse_allowed = (which[None, :] == every_which[:, None]) & (
            places[None, :] <= every_place[:, None]
        )
        back_scores = scores_of(query_all, key_rows, reverse_allowed)
        back_probs = jnp.exp(back_scores - top_all) / total_all
        back_d_probs = jnp.einsum("thd,jhd->htj", d_att_all, value_rows, preferred_element_type=f32)
        back_d_scores = (back_probs * (back_d_probs - delta_all)).astype(bf16)
        d_key = (
            jnp.einsum("htj,thd->jhd", back_d_scores, query_all, preferred_element_type=f32)
            * factor
        )
        d_value = jnp.einsum(
            "htj,thd->jhd", back_probs.astype(bf16), d_att_all, preferred_element_type=f32
        )
        d_query = rope_turn(d_query.reshape(rows, D), places, -1.0)
        d_key = rope_turn(d_key.reshape(rows, D), places, -1.0)
        d_mixed = jnp.concatenate([d_query, d_key, d_value.reshape(rows, D)], axis=1).astype(bf16)
        g_qkv = jnp.dot(normal_a.T, d_mixed, preferred_element_type=f32)
        d_normal_a = jnp.dot(d_mixed, w_qkv[layer].T, preferred_element_type=f32)
        d_in, d_gain_a = jax.vjp(normed, resid_in, gains[layer, 0])[1](d_normal_a)
        grad = grad + d_in
        terms = (g_qkv, g_out, g_gate_up, g_down, jnp.stack([d_gain_a, d_gain_b]))
        layer_terms[layer] = terms
    d_first = grad.astype(bf16)
    g_lag = jnp.dot(feats.T, d_first, preferred_element_type=f32)
    d_feats = jnp.dot(d_first, w_lag.T, preferred_element_type=f32)
    d_extended = feature_back(d_feats)[0]
    raw_grad = d_extended[MAXLAG:]
    for step in range(1, HALO_BLOCKS + 1):
        piece = d_extended[(HALO_BLOCKS - step) * rows : (HALO_BLOCKS - step + 1) * rows]
        raw_grad = raw_grad + shifted(piece[None], "tm", -step)[0]
    labels = jnp.arange(DATASETS, dtype=jnp.int32)
    member = (dataset_ids[0, :, 0][:, None] == labels[None, :]).astype(f32)
    owner = (lax.axis_index("tm") == 0).astype(f32)
    scale_sums = jnp.sum(member * scales[:, None], axis=0) * owner
    counts = jnp.sum(member, axis=0) * owner
    stacked = tuple(
        (
            jnp.stack([layer_terms[layer][member_index] for layer in range(LAYERS)])
            for member_index in range(5)
        )
    )
    g_lag, g_qkv_all, g_out_all, g_gate_up_all, g_down_all, g_gains_all, scale_sums, counts = (
        lax.psum(
            (g_lag, stacked[0], stacked[1], stacked[2], stacked[3], stacked[4], scale_sums, counts),
            ("series", "tm"),
        )
    )
    return (
        resid[None],
        raw_grad[None],
        scale_sums / counts,
        g_lag,
        g_qkv_all,
        g_out_all,
        g_gate_up_all,
        g_down_all,
        g_gains_all,
    )


def solution(mesh):
    placed = (
        P("series", "tm"),
        P("series", "tm"),
        P("series", None),
        P("series", None),
        P("series", None, None),
        P(),
        P(),
        P(),
        P(),
        P(),
        P(),
        P(),
        P("series", "tm", None),
    )
    return jax.shard_map(
        body,
        mesh=mesh,
        in_specs=placed,
        out_specs=(P("series", "tm", None), P("series", "tm"), P(), P(), P(), P(), P(), P(), P()),
        check_vma=False,
    )
```

profile of v0, /device:TPU:1, one launch (start us, length us, event | category | flops | bytes accessed | tf_op | source)
XLA Modules:
  0.0 636.6 jit_solution(6525009580366169807)
XLA Ops:
  7.2 4.0 collective-permute-start.1
  11.3 5.4 collective-permute-start
  16.6 1.9 collective-permute-start.2
  25.4 63.1 %gather_fusion = f32[10752]{0:T(1024)S(1)} fusion(f32[512]{0:T(512)S(1)} %bitcast.217, s32[11264]{0:T(1024)S(1)} %pad_clamp_fusion), kind=kCustom, calls=%fused_computation | custom fusion | bytes 129024 | tf_op jit(solution)/shard_map/jvp(jit(_take))/gather | solution.py:51
  91.5 45.9 %all-gather.5.cloned.1.call-done = bf16[4096,18,16]{0,2,1:T(8,128)(2,1)} async-done(((bf16[128,18,16]{0,2,1:T(8,128)(2,1)}), bf16[4096,18,16]{0,2,1:T(8,128)(2,1)}) %all-gather.5.cloned.1.call-update) | async-done | bytes 2359312 | tf_op jit(solution)/shard_map/all_gather | solution.py:30
  137.5 10.8 %fusion = (f32[9,128]{1,0:T(8,128)S(1)}, f32[9,128,4096]{2,1,0:T(8,128)}) fusion(pred[128,4096]{1,0:T(8,128)(4,1)S(1)} %fusion.22, bf16[4096,18,16]{0,2,1:T(8,128)(2,1)} %all-gather.5.cloned.1.call-done, bf16[128,9,8]{0,2,1:T(8,128)(2,1)S(1)} %get-tuple-element.57, bf16[128,9,8]{0,2,1:T(8,128)(2,1)S(1)} %get-tuple-element.56), kind=kOutput, calls=%fused_computation.14 | convolution fusion | flops 165223296 | bytes 20619776 | tf_op jit(solution)/shard_map/thd,jhd->htj/dot_general | solution.py:87
  148.9 11.7 %fusion.3 = f32[9,128]{1,0:T(8,128)} fusion(f32[9,128,4096]{2,1,0:T(8,128)} %get-tuple-element.83, f32[9,128]{1,0:T(8,128)S(1)} %get-tuple-element.82, pred[128,4096]{1,0:T(8,128)(4,1)S(1)} %fusion.22), kind=kLoop, calls=%fused_computation.17 | loop fusion | flops 18873216 | bytes 19407872 | tf_op jit(solution)/shard_map/reduce_sum | solution.py:145
  160.6 8.9 %fusion.41 = bf16[9,16,128]{2,1,0:T(8,128)(2,1)S(1)} fusion(bf16[4096,18,16]{0,2,1:T(8,128)(2,1)S(1)} %copy-done.26, f32[9,128,4096]{2,1,0:T(8,128)} %get-tuple-element.83, f32[9,128]{1,0:T(8,128)} %fusion.3, f32[9,128]{1,0:T(8,128)} %copy-done.56, pred[128,4096]{1,0:T(8,128)(4,1)S(1)} %fusion.22), kind=kOutput, calls=%fused_computation.69 | convolution fusion | flops 174606336 | bytes 21804032 | tf_op jit(solution)/shard_map/htj,jhd->thd/dot_general | solution.py:148
  175.4 3.2 fusion.23
  178.6 39.9 %all-gather.7.cloned.1.call-done = bf16[4096,18,16]{0,2,1:T(8,128)(2,1)} async-done(((bf16[128,18,16]{0,2,1:T(8,128)(2,1)}), bf16[4096,18,16]{0,2,1:T(8,128)(2,1)}) %all-gather.7.cloned.1.call-update) | async-done | bytes 2359312 | tf_op jit(solution)/shard_map/all_gather | solution.py:30
  218.4 10.9 %fusion.1 = (f32[9,128]{1,0:T(8,128)S(1)}, f32[9,128,4096]{2,1,0:T(8,128)}) fusion(pred[128,4096]{1,0:T(8,128)(4,1)S(1)} %fusion.22, bf16[4096,18,16]{0,2,1:T(8,128)(2,1)} %all-gather.7.cloned.1.call-done, bf16[128,9,8]{0,2,1:T(8,128)(2,1)} %get-tuple-element.53, bf16[128,9,8]{0,2,1:T(8,128)(2,1)} %get-tuple-element.52), kind=kOutput, calls=%fused_computation.15 | convolution fusion | flops 165223296 | bytes 20619776 | tf_op jit(solution)/shard_map/thd,jhd->htj/dot_general | solution.py:87
  229.4 11.7 %fusion.5 = f32[9,128]{1,0:T(8,128)} fusion(f32[9,128,4096]{2,1,0:T(8,128)} %get-tuple-element.89, f32[9,128]{1,0:T(8,128)S(1)} %get-tuple-element.88, pred[128,4096]{1,0:T(8,128)(4,1)S(1)} %fusion.22), kind=kLoop, calls=%fused_computation.19 | loop fusion | flops 18873216 | bytes 19407872 | tf_op jit(solution)/shard_map/reduce_sum | solution.py:145
  241.1 9.1 %fusion.44 = bf16[9,16,128]{2,1,0:T(8,128)(2,1)S(1)} fusion(bf16[4096,18,16]{0,2,1:T(8,128)(2,1)S(1)} %copy-done.27, f32[9,128,4096]{2,1,0:T(8,128)} %get-tuple-element.89, f32[9,128]{1,0:T(8,128)} %fusion.5, f32[9,128]{1,0:T(8,128)S(1)} %get-tuple-element.88, pred[128,4096]{1,0:T(8,128)(4,1)S(1)} %fusion.22), kind=kOutput, calls=%fused_computation.70 | convolution fusion | flops 174606336 | bytes 21804032 | tf_op jit(solution)/shard_map/htj,jhd->thd/dot_general | solution.py:148
  256.5 17.5 %multiply_reduce_fusion.1 = (f32[9,128]{1,0:T(8,128)S(1)}, f32[9,128,4096]{2,1,0:T(8,128)}) fusion(f32[9,128]{1,0:T(8,128)} %fusion.5, f32[9,128]{1,0:T(8,128)S(1)} %get-tuple-element.88, f32[9,128,4096]{2,1,0:T(8,128)} %get-tuple-element.89, pred[128,4096]{1,0:T(8,128)(4,1)S(1)} %fusion.22, bf16[128,9,16]{0,2,1:T(8,128)(2,1)S(1)} %bitcast.243, ...), kind=kOutput, calls=%fused_computation.9 | convolution fusion | flops 179305344 | bytes 39506944 | tf_op jit(solution)/shard_map/thd,jhd->htj/dot_general | solution.py:213
  274.1 24.4 %all_gather.21 = f32[27,4096,1]{1,0,2:T(8,128)S(1)} all-gather(f32[27,128,1]{1,0,2:T(8,128)S(1)} %pad_maximum_fusion.19), channel_id=1, replica_groups=mesh['series'=4,'tm'=32] {'tm'}, dimensions={1}, use_global_device_ids=true | all-gather | bytes 456192 | tf_op jit(solution)/shard_map/all_gather | solution.py:30
  299.3 15.5 %fusion.35 = f32[128,9,16]{0,2,1:T(8,128)} fusion(bf16[4096,18,16]{0,2,1:T(8,128)(2,1)S(1)} %copy-done.27, f32[9,128,4096]{2,1,0:T(8,128)} %get-tuple-element.94, f32[9,128]{1,0:T(8,128)S(1)} %get-tuple-element.93, f32[9,128,4096]{2,1,0:T(8,128)} %get-tuple-element.89, f32[9,128]{1,0:T(8,128)S(1)} %copy-done.72, f32[9,128]{1,0:T(8,128)S(1)} %get-tuple-element.88, ...), kind=kOutput, calls=%fused_computation.59 | convolution fusion | flops 184043520 | bytes 40719872 | tf_op jit(solution)/shard_map/htj,jhd->thd/dot_general | solution.py:216
  314.9 10.8 %fusion.169 = f32[9,4096,128]{2,1,0:T(8,128)} fusion(bf16[4096,18,16]{0,2,1:T(8,128)(2,1)} %all-gather.9.cloned.1.call-done, bf16[128,9,16]{0,2,1:T(8,128)(2,1)} %bitcast.237), kind=kOutput, calls=%fused_computation.300 | convolution fusion | flops 150994944 | bytes 21270528 | tf_op jit(solution)/shard_map/thd,jhd->htj/dot_general | solution.py:224
  325.8 12.6 %exponential_divide_fusion.1 = f32[9,4096,128]{2,1,0:T(8,128)S(1)} fusion(bf16[4096,18,16]{0,2,1:T(8,128)(2,1)S(1)} %copy-done.3, f32[9,4096]{1,0:T(8,128)S(1)} %get-tuple-element.37, f32[9,4096]{1,0:T(8,128)S(1)} %copy-done.34, pred[4096,128]{1,0:T(8,128)(4,1)S(1)} %copy-done.28, bf16[128,9,8]{0,2,1:T(8,128)(2,1)S(1)} %copy-done.63, ...), kind=kOutput, calls=%fused_computation.7 | convolution fusion | flops 169943040 | bytes 22089728 | tf_op jit(solution)/shard_map/thd,jhd->htj/dot_general | solution.py:87
  338.4 15.4 %fusion.40 = f32[128,9,16]{0,2,1:T(8,128)S(1)} fusion(bf16[4096,18,16]{0,2,1:T(8,128)(2,1)S(1)} %copy-done.3, f32[9,4096,128]{2,1,0:T(8,128)S(1)} %exponential_divide_fusion.1, f32[9,4096,128]{2,1,0:T(8,128)} %fusion.169, f32[9,4096]{1,0:T(8,128)S(1)} %get-tuple-element.36), kind=kOutput, calls=%fused_computation.68 | convolution fusion | flops 165169152 | bytes 40329216 | tf_op jit(solution)/shard_map/htj,thd->jhd/dot_general | solution.py:227
  354.1 7.9 %fusion.47 = bf16[9,16,128]{2,1,0:T(8,128)(2,1)S(1)} fusion(bf16[4096,18,16]{0,2,1:T(8,128)(2,1)S(1)} %copy-done.3, f32[9,4096,128]{2,1,0:T(8,128)} %copy-done.1), kind=kOutput, calls=%fused_computation.71 | convolution fusion | flops 155731968 | bytes 21270528 | tf_op jit(solution)/shard_map/htj,thd->jhd/dot_general | solution.py:230
  366.4 14.8 %multiply_reduce_fusion = (f32[9,128]{1,0:T(8,128)S(1)}, f32[9,128,4096]{2,1,0:T(8,128)}) fusion(f32[9,128]{1,0:T(8,128)S(1)} %copy-done.71, f32[9,128]{1,0:T(8,128)S(1)} %copy-done.57, f32[9,128,4096]{2,1,0:T(8,128)} %get-tuple-element.83, pred[128,4096]{1,0:T(8,128)(4,1)S(1)} %fusion.22, bf16[128,9,16]{0,2,1:T(8,128)(2,1)S(1)} %bitcast.245, ...), kind=kOutput, calls=%fused_computation.5 | convolution fusion | flops 179305344 | bytes 39503360 | tf_op jit(solution)/shard_map/thd,jhd->htj/dot_general | solution.py:213
  381.2 23.2 %all_gather.23 = f32[27,4096,1]{1,0,2:T(8,128)S(1)} all-gather(f32[27,128,1]{1,0,2:T(8,128)S(1)} %pad_maximum_fusion.20), channel_id=1, replica_groups=mesh['series'=4,'tm'=32] {'tm'}, dimensions={1}, use_global_device_ids=true | all-gather | bytes 456192 | tf_op jit(solution)/shard_map/all_gather | solution.py:30
  407.0 15.6 %fusion.33 = f32[128,9,16]{0,2,1:T(8,128)S(1)} fusion(bf16[4096,18,16]{0,2,1:T(8,128)(2,1)} %all-gather.5.cloned.1.call-done, f32[9,128,4096]{2,1,0:T(8,128)} %get-tuple-element.98, f32[9,128]{1,0:T(8,128)S(1)} %get-tuple-element.97, f32[9,128,4096]{2,1,0:T(8,128)} %get-tuple-element.83, f32[9,128]{1,0:T(8,128)S(1)} %copy-done.71, ...), kind=kOutput, calls=%fused_computation.57 | convolution fusion | flops 184043520 | bytes 40719872 | tf_op jit(solution)/shard_map/htj,jhd->thd/dot_general | solution.py:216
  422.6 10.8 %fusion.170 = f32[9,4096,128]{2,1,0:T(8,128)} fusion(bf16[4096,18,16]{0,2,1:T(8,128)(2,1)} %all-gather.11.cloned.1.call-done, bf16[128,9,16]{0,2,1:T(8,128)(2,1)S(1)} %bitcast.235), kind=kOutput, calls=%fused_computation.301 | convolution fusion | flops 150994944 | bytes 21270528 | tf_op jit(solution)/shard_map/thd,jhd->htj/dot_general | solution.py:224
  433.4 12.6 %exponential_divide_fusion = f32[9,4096,128]{2,1,0:T(8,128)S(1)} fusion(bf16[4096,18,16]{0,2,1:T(8,128)(2,1)S(1)} %copy-done.2, f32[9,4096]{1,0:T(8,128)S(1)} %get-tuple-element.34, f32[9,4096]{1,0:T(8,128)S(1)} %get-tuple-element.35, pred[4096,128]{1,0:T(8,128)(4,1)S(1)} %copy-done.28, bf16[128,9,8]{0,2,1:T(8,128)(2,1)S(1)} %copy-done.59, ...), kind=kOutput, calls=%fused_computation.3 | convolution fusion | flops 169943040 | bytes 22089728 | tf_op jit(solution)/shard_map/thd,jhd->htj/dot_general | solution.py:87
  446.1 15.1 %fusion.38 = f32[128,9,16]{0,2,1:T(8,128)S(1)} fusion(bf16[4096,18,16]{0,2,1:T(8,128)(2,1)S(1)} %copy-done.2, f32[9,4096,128]{2,1,0:T(8,128)S(1)} %exponential_divide_fusion, f32[9,4096,128]{2,1,0:T(8,128)} %fusion.170, f32[9,4096]{1,0:T(8,128)S(1)} %get-tuple-element.33), kind=kOutput, calls=%fused_computation.66 | convolution fusion | flops 165169152 | bytes 40329216 | tf_op jit(solution)/shard_map/htj,thd->jhd/dot_general | solution.py:227
  461.5 7.8 %fusion.50 = bf16[9,16,128]{2,1,0:T(8,128)(2,1)S(1)} fusion(bf16[4096,18,16]{0,2,1:T(8,128)(2,1)S(1)} %copy-done.2, f32[9,4096,128]{2,1,0:T(8,128)} %copy-done), kind=kOutput, calls=%fused_computation.72 | convolution fusion | flops 155731968 | bytes 21270528 | tf_op jit(solution)/shard_map/htj,thd->jhd/dot_general | solution.py:230
  471.4 75.0 %scatter_custom_fusion = f32[512]{0:T(512)S(1)} fusion(s32[10752]{0:T(1024)} %copy-done.40, f32[10752]{0:T(1024)S(1)} %reshape.532, f32[]{:T(128)} %constant.62.clone.1), kind=kCustom, calls=%fused_computation.251 | custom fusion | flops 10752 | bytes 2560 | tf_op jit(solution)/shard_map/transpose(jvp(jit(_take)))/scatter-add | solution.py:51
  546.4 2.1 collective-permute-start.3
  551.3 69.9 %all-reduce.4 = (f32[8]{0:T(128)S(1)}, f32[8]{0:T(128)S(1)}, f32[87,144]{0,1:T(8,128)}, f32[2,2,144]{2,1,0:T(2,128)}) all-reduce(f32[8]{0:T(128)S(1)} %copy-done.102, f32[8]{0:T(128)S(1)} %copy-done.101, f32[87,144]{0,1:T(8,128)S(1)} %fusion.135, ...), channel_id=1, replica_groups=mesh['series'=4,'tm'=32] {'series','tm'}, use_global_device_ids=true, to_apply=%region_21.22 | all-reduce | flops 13120 | bytes 104960 | tf_op jit(solution)/shard_map/psum | solution.py:262
  622.3 1.9 copy.30
  625.9 2.1 copy.32
  (338 shorter events, 39.0 us)
Async XLA Ops:
  7.2 130.3 %all-gather.5.cloned.1.call-start = ((), (), s32[]{:S(2)}) async-start(), calls=%async_computation | async-start | bytes 2433024 | tf_op jit(solution)/shard_map/all_gather | solution.py:30
  7.2 17.4 %collective-permute-start.1 = (f32[1,128]{1,0:T(1,128)}, f32[1,128]{1,0:T(1,128)S(1)}, u32[]{:S(2)}, u32[]{:S(2)}) collective-permute-start(f32[1,128]{1,0:T(1,128)} %param.13), channel_id=1, source_target_pairs={{0,2},{1,3},{2,4},{3,5},{4,6},{5,7},{6,8},{7,9},{8,10},{9,11},{10,... | collective-permute-start | bytes 1544 | tf_op jit(solution)/shard_map/ppermute | solution.py:25
  11.3 13.4 %collective-permute-start = (f32[1,128]{1,0:T(1,128)}, f32[1,128]{1,0:T(1,128)S(1)}, u32[]{:S(2)}, u32[]{:S(2)}) collective-permute-start(f32[1,128]{1,0:T(1,128)} %param.13), channel_id=1, source_target_pairs={{0,3},{1,4},{2,5},{3,6},{4,7},{5,8},{6,9},{7,10},{8,11},{9,12},{10... | collective-permute-start | bytes 1544 | tf_op jit(solution)/shard_map/ppermute | solution.py:25
  16.6 8.0 %collective-permute-start.2 = (f32[1,128]{1,0:T(1,128)}, f32[1,128]{1,0:T(1,128)S(1)}, u32[]{:S(2)}, u32[]{:S(2)}) collective-permute-start(f32[1,128]{1,0:T(1,128)} %param.13), channel_id=1, source_target_pairs={{0,1},{1,2},{2,3},{3,4},{4,5},{5,6},{6,7},{7,8},{8,9},{9,10},{10,1... | collective-permute-start | bytes 1544 | tf_op jit(solution)/shard_map/ppermute | solution.py:25
  18.6 71.8 %copy-start.82 = (s32[128]{0:T(128)}, s32[128]{0:T(128)S(1)}, u32[]{:S(2)}) copy-start(s32[128]{0:T(128)S(1)} %get-tuple-element.100) | copy-start | bytes 1540
  19.3 69.5 %copy-start.93 = (bf16[128,1]{0,1:T(2,128)(2,1)}, bf16[128,1]{0,1:T(2,128)(2,1)S(1)}, u32[]{:S(2)}) copy-start(bf16[128,1]{0,1:T(2,128)(2,1)S(1)} %get-tuple-element.78) | copy-start | bytes 772
  19.3 69.5 %copy-start.95 = (bf16[128,1]{0,1:T(2,128)(2,1)}, bf16[128,1]{0,1:T(2,128)(2,1)S(1)}, u32[]{:S(2)}) copy-start(bf16[128,1]{0,1:T(2,128)(2,1)S(1)} %get-tuple-element.79) | copy-start | bytes 772
  20.7 68.4 %copy-start.76 = (f32[1,1,144]{2,1,0:T(1,128)}, f32[1,1,144]{2,1,0:T(1,128)S(1)}, u32[]{:S(2)}) copy-start(f32[1,1,144]{2,1,0:T(1,128)S(1)} %get-tuple-element.70) | copy-start | bytes 1732
  23.1 65.5 %copy-start.99 = (s32[128]{0:T(128)}, s32[128]{0:T(128)S(1)}, u32[]{:S(2)}) copy-start(s32[128]{0:T(128)S(1)} %get-tuple-element.17) | copy-start | bytes 1540
  23.2 67.3 %copy-start.88 = (s32[128]{0:T(128)}, s32[128]{0:T(128)S(1)}, u32[]{:S(2)}) copy-start(s32[128]{0:T(128)S(1)} %get-tuple-element.18) | copy-start | bytes 1540
  23.9 64.8 %copy-start.103 = (f32[128]{0:T(128)}, f32[128]{0:T(128)S(1)}, u32[]{:S(2)}) copy-start(f32[128]{0:T(128)S(1)} %select_reduce_fusion.1) | copy-start | bytes 1540
  24.6 147.0 %copy-start.53 = (f32[128,8]{0,1:T(8,128)}, f32[128,8]{0,1:T(8,128)S(1)}, u32[]{:S(2)}) copy-start(f32[128,8]{0,1:T(8,128)S(1)} %get-tuple-element.77) | copy-start | bytes 12292
  24.6 64.2 %copy-start.97 = (bf16[128,1]{0,1:T(2,128)(2,1)}, bf16[128,1]{0,1:T(2,128)(2,1)S(1)}, u32[]{:S(2)}) copy-start(bf16[128,1]{0,1:T(2,128)(2,1)S(1)} %convert_bitcast_fusion) | copy-start | bytes 772
  25.3 63.4 %copy-start.91 = (s32[84]{0:T(128)S(1)}, s32[84]{0:T(128)}, u32[]{:S(2)}) copy-start(s32[84]{0:T(128)} %param.18) | copy-start | bytes 1012
  25.3 63.5 %copy-start.69 = (bf16[87,144]{0,1:T(8,128)(2,1)S(1)}, bf16[87,144]{0,1:T(8,128)(2,1)}, u32[]{:S(2)}) copy-start(bf16[87,144]{0,1:T(8,128)(2,1)} %param.19) | copy-start | bytes 75172
  25.3 63.7 %copy-start.29 = (bf16[2,144,432]{2,1,0:T(8,128)(2,1)S(1)}, bf16[2,144,432]{2,1,0:T(8,128)(2,1)}, u32[]{:S(2)}) copy-start(bf16[2,144,432]{2,1,0:T(8,128)(2,1)} %param.20) | copy-start | bytes 746500
  89.0 80.6 %copy-start.6 = (f32[128,144]{0,1:T(8,128)}, f32[128,144]{0,1:T(8,128)S(1)}, u32[]{:S(2)}) copy-start(f32[128,144]{0,1:T(8,128)S(1)} %get-tuple-element.81) | copy-start | bytes 221188
  90.2 128.3 %all-gather.7.cloned.1.call-start = ((), (), s32[]{:S(2)}) async-start(), calls=%async_computation.1 | async-start | bytes 2433024 | tf_op jit(solution)/shard_map/all_gather | solution.py:30
  171.2 79.0 %copy-start.8 = (f32[128,144]{0,1:T(8,128)}, f32[128,144]{0,1:T(8,128)S(1)}, u32[]{:S(2)}) copy-start(f32[128,144]{0,1:T(8,128)S(1)} %get-tuple-element.87) | copy-start | bytes 221188
  173.5 141.3 %all-gather.9.cloned.1.call-start = ((), (), s32[]{:S(2)}) async-start(), calls=%async_computation.2 | async-start | bytes 2433024 | tf_op jit(solution)/shard_map/all_gather | solution.py:30
  256.5 166.1 %all-gather.11.cloned.1.call-start = ((), (), s32[]{:S(2)}) async-start(), calls=%async_computation.3 | async-start | bytes 2433024 | tf_op jit(solution)/shard_map/all_gather | solution.py:30
  366.3 256.0 %all-reduce.8.cloned.1.call-start = ((), (), s32[]{:S(2)}) async-start(), calls=%async_computation.4 | async-start | bytes 4423680 | tf_op jit(solution)/shard_map/psum | solution.py:262
  461.4 89.7 %copy-start.89 = (f32[144]{0:T(256)S(1)}, f32[144]{0:T(256)}, u32[]{:S(2)}) copy-start(f32[144]{0:T(256)} %get-tuple-element.11) | copy-start | bytes 1732
  461.4 89.7 %copy-start.39 = (bf16[128,84]{0,1:T(8,128)(2,1)S(1)}, bf16[128,84]{0,1:T(8,128)(2,1)}, u32[]{:S(2)}) copy-start(bf16[128,84]{0,1:T(8,128)(2,1)} %copy-done.38) | copy-start | bytes 64516
  461.4 89.7 %copy-start.94 = (bf16[128,1]{0,1:T(2,128)(2,1)S(1)}, bf16[128,1]{0,1:T(2,128)(2,1)}, u32[]{:S(2)}) copy-start(bf16[128,1]{0,1:T(2,128)(2,1)} %copy-done.93) | copy-start | bytes 772
  461.4 89.7 %copy-start.96 = (bf16[128,1]{0,1:T(2,128)(2,1)S(1)}, bf16[128,1]{0,1:T(2,128)(2,1)}, u32[]{:S(2)}) copy-start(bf16[128,1]{0,1:T(2,128)(2,1)} %copy-done.95) | copy-start | bytes 772
  461.4 89.7 %copy-start.98 = (bf16[128,1]{0,1:T(2,128)(2,1)S(1)}, bf16[128,1]{0,1:T(2,128)(2,1)}, u32[]{:S(2)}) copy-start(bf16[128,1]{0,1:T(2,128)(2,1)} %copy-done.97) | copy-start | bytes 772
  461.4 89.9 %copy-start.101 = (f32[8]{0:T(128)S(1)}, f32[8]{0:T(128)}, u32[]{:S(2)}) copy-start(f32[8]{0:T(128)} %get-tuple-element.102) | copy-start | bytes 100
  461.4 89.9 %copy-start.102 = (f32[8]{0:T(128)S(1)}, f32[8]{0:T(128)}, u32[]{:S(2)}) copy-start(f32[8]{0:T(128)} %get-tuple-element.103) | copy-start | bytes 100
  546.4 75.4 %collective-permute-start.3 = (f32[1,128]{1,0:T(1,128)S(1)}, f32[1,128]{1,0:T(1,128)S(1)}, u32[]{:S(2)}, u32[]{:S(2)}) collective-permute-start(f32[1,128]{1,0:T(1,128)S(1)} %get-tuple-element.72), channel_id=1, source_target_pairs={{1,0},{2,1},{3,2},{4,3},{5,4},{6,5},{7,6},{8,7},{9,8},{10,9},{11,1... | collective-permute-start | bytes 1544 | tf_op jit(solution)/shard_map/ppermute | solution.py:25
  548.5 73.3 %collective-permute-start.5 = (f32[1,128]{1,0:T(1,128)S(1)}, f32[1,128]{1,0:T(1,128)S(1)}, u32[]{:S(2)}, u32[]{:S(2)}) collective-permute-start(f32[1,128]{1,0:T(1,128)S(1)} %get-tuple-element.73), channel_id=1, source_target_pairs={{3,0},{4,1},{5,2},{6,3},{7,4},{8,5},{9,6},{10,7},{11,8},{12,9},{13... | collective-permute-start | bytes 1544 | tf_op jit(solution)/shard_map/ppermute | solution.py:25
  549.8 72.0 %collective-permute-start.4 = (f32[1,128]{1,0:T(1,128)S(1)}, f32[1,128]{1,0:T(1,128)S(1)}, u32[]{:S(2)}, u32[]{:S(2)}) collective-permute-start(f32[1,128]{1,0:T(1,128)S(1)} %get-tuple-element.74), channel_id=1, source_target_pairs={{2,0},{3,1},{4,2},{5,3},{6,4},{7,5},{8,6},{9,7},{10,8},{11,9},{12,... | collective-permute-start | bytes 1544 | tf_op jit(solution)/shard_map/ppermute | solution.py:25
  (90 other events, 1097.3 us)
Sparse Core Ops, SparseCore 0:
  90.3 47.1 all-gather.4
  173.7 44.7 all-gather.6
  256.6 45.6 all-gather.8
  366.4 44.8 all-gather.10
  471.0 151.0 all-reduce.7
where the time goes:
time: 647 us; the launch traced here: 637 us
  matrix products  207 us (32%)
  blocking collectives  118 us (18%)
  other arithmetic  117 us (18%)
  waiting for transfers between devices  85.9 us (13%)
  local copies, waits for them, and re-layouts  76.3 us (12%)
  starting transfers between devices  16.7 us (3%)
  between operations  15.9 us (2%)
    all_gather x4, waiting for transfers between devices, side_by_side(): out, at, done = (lax.all_gather(both, axis, axis=dim, tiled=True), 0, [])  85.8 us
    scatter-add x1, other arithmetic, lag_features(): lagged = jnp.take(extended, index)  75 us
    psum x1, blocking collectives, body(): lax.psum((g_lag, stacked[0], stacked[1], stacked[2], stacked[3], stacked[...  69.9 us
    gather x3, local copies, waits for them, and re-layouts, lag_features(): lagged = jnp.take(extended, index)  63.3 us
    all_gather x2, blocking collectives, side_by_side(): out, at, done = (lax.all_gather(both, axis, axis=dim, tiled=True), 0, [])  47.6 us
    dot_general x4, matrix products, scores_of(): jnp.einsum('thd,jhd->htj', queries, keys, preferred_element_type=jnp.floa...  47 us
    dot_general x2, matrix products, body(): jnp.einsum('thd,jhd->htj', d_att, value_all, preferred_element_type=f32)  32.4 us
    dot_general x2, matrix products, body(): jnp.einsum('htj,jhd->thd', d_scores, key_all, preferred_element_type=f32)  31.1 us
  transfers between devices with their start and end apart: 11, of which 2 were waited for; matrix products, arithmetic and copies ran while one was open for 24% of the time, Pallas kernels for 0%

commit v1 on v0

v1 whole, which is shorter than its diff:
```python
import math

import jax
import jax.numpy as jnp
import numpy as np
from jax import lax
from jax.experimental import pallas as pl
from jax.experimental.pallas import tpu as pltpu
from jax.sharding import PartitionSpec as P


D = 144
HEADS = 9
HEAD_DIM = 16
FF = 384
LAGS = 84
LAYERS = 2
DATASETS = 8
DOCS = 7
LEN = 4096
MAXLAG = 384
FEATS = 87
EPSILON = 1e-06
MASKED = -1e30
AUG = 192
STAT = AUG - D
LROW = D
DROW = D + 27
BLOCK = 512
BLOCKS = LEN // BLOCK
TILE = 128
TILES = LEN // TILE
STEPS = BLOCKS + 1
HALF = 64
ROWS = HEADS * HALF
LAGCOLS = 400
VMEM = 56 * 2**20

bf16 = jnp.bfloat16
f32 = jnp.float32
HIGH = lax.Precision.HIGHEST


def nn(a, b, precision=None):
    return lax.dot_general(a, b, (((1,), (0,)), ((), ())), precision=precision, preferred_element_type=f32)


def nt(a, b, precision=None):
    return lax.dot_general(a, b, (((1,), (1,)), ((), ())), precision=precision, preferred_element_type=f32)


def tn(a, b, precision=None):
    return lax.dot_general(a, b, (((0,), (0,)), ((), ())), precision=precision, preferred_element_type=f32)


def iota(shape, dim):
    return lax.broadcasted_iota(jnp.int32, shape, dim)


def eye(rows, cols, dtype):
    return (iota((rows, cols), 0) == iota((rows, cols), 1)).astype(dtype)


def column(row, size):
    keep = iota((size, size), 0) == iota((size, size), 1)
    return jnp.sum(jnp.where(keep, row, 0.0), axis=1, keepdims=True)


def geometry():
    index = lax.axis_index("tm")
    chip, core = index // 2, index % 2
    low = jnp.where(core == 0, chip, TILES - 1 - chip)
    return chip, core, low, TILES - 1 - low


def doc_start(places, len_ref):
    start = jnp.zeros_like(places)
    end = jnp.int32(0)
    for d in range(DOCS):
        end = end + len_ref[d]
        start = jnp.where(places >= end, end, start)
    return start


def doc_scale_at(places, len_ref, scale_ref):
    own = jnp.full(places.shape, scale_ref[0], f32)
    end = jnp.int32(0)
    for d in range(1, DOCS):
        end = end + len_ref[d - 1]
        own = jnp.where(places >= end, scale_ref[d], own)
    return own


def own_places(low, high):
    lane = iota((1, TILE), 1)
    return jnp.where(lane < HALF, low, high) * TILE + lane


def half_places(u, tile):
    return iota((HALF, 1), 0) + (tile * TILE + u * HALF)


def rotate(x, cosine, sine):
    cols = x.shape[1]
    parts = x.reshape(HEADS, 2, 8, cols)
    one, two = parts[:, 0], parts[:, 1]
    turned = jnp.stack([one * cosine - two * sine, two * cosine + one * sine], axis=1)
    return turned.reshape(D, cols)


def norm_factor(x):
    return lax.rsqrt(jnp.mean(x * x, axis=0, keepdims=True) + EPSILON)


def norm_back(x, gain, d_normal):
    r = norm_factor(x)
    scaled = d_normal * gain
    inner = jnp.mean(x * scaled, axis=0, keepdims=True)
    d_x = r * scaled - (r * r * r * inner) * x
    return d_x, jnp.sum(d_normal * x * r, axis=1, keepdims=True)


def head_columns(h, *firsts):
    col = iota((1, AUG), 1)
    keep = (col >= h * HEAD_DIM) & (col < (h + 1) * HEAD_DIM)
    for first in firsts:
        keep = keep | (col == first + h)
    return keep


def spread(ref, rows, *firsts):
    zero = jnp.zeros((HALF, AUG), f32)
    for h in range(HEADS):
        keep = head_columns(h, *firsts)
        for u in range(2):
            part = rows[u * HALF : (u + 1) * HALF]
            ref[u, h * HALF : (h + 1) * HALF, :] = jnp.where(keep, part, zero).astype(bf16)


def own_heads(x):
    col = iota((1, D), 1) // HEAD_DIM
    total = jnp.zeros((HALF, D), f32)
    for h in range(HEADS):
        total = jnp.where(col == h, x[h * HALF : (h + 1) * HALF, :D], total)
    return total


def three_parts(x):
    hi = x.astype(bf16)
    rest = x - hi.astype(f32)
    mid = rest.astype(bf16)
    return hi, mid, (rest - mid.astype(f32)).astype(bf16)


def put_tiles(ref, first, grads):
    at = first
    for c in range(grads.shape[1] // TILE):
        for r in range(grads.shape[0] // 16):
            ref[at] = grads[16 * r : 16 * (r + 1), c * TILE : (c + 1) * TILE].astype(bf16)
            at += 1
    return at


def qkv_block(normal, w_qkv, rope_ref, k, kaug_ref, vaug_ref, qall_ref):
    mixed = tn(w_qkv, normal)
    cosine = rope_ref[0:8, k * BLOCK : (k + 1) * BLOCK]
    sine = rope_ref[8:16, k * BLOCK : (k + 1) * BLOCK]
    qall_ref[k] = (rotate(mixed[:D], cosine, sine).astype(bf16).astype(f32) * HEAD_DIM**-0.5).astype(bf16)
    kaug_ref[k, 0:D, :] = rotate(mixed[D : 2 * D], cosine, sine).astype(bf16)
    vaug_ref[k, 0:D, :] = mixed[2 * D :].astype(bf16)
    ones = jnp.ones((STAT, BLOCK), bf16)
    kaug_ref[k, D:AUG, :] = ones
    vaug_ref[k, D:AUG, :] = ones


def own_tile(ref, low, high):
    lane = iota((1, TILE), 1)

    def at(tile):
        return ref[tile // 4, 0:D, pl.ds(pl.multiple_of((tile % 4) * TILE, TILE), TILE)].astype(f32)

    return jnp.where(lane < HALF, at(low), at(high)).astype(bf16)


def query_bias(u, tile, block, len_ref):
    places = half_places(u, tile)
    start = doc_start(places, len_ref)
    keys = iota((1, BLOCK), 1) + block * BLOCK
    return jnp.where((keys <= places) & (keys >= start), 0.0, MASKED)


def key_bias(u, tile, block, len_ref):
    keys = half_places(u, tile)
    places = iota((1, BLOCK), 1) + block * BLOCK
    start = doc_start(places, len_ref)
    return jnp.where((keys <= places) & (keys >= start), 0.0, MASKED)


def biased(scores, bias):
    return (scores.reshape(HEADS, HALF, BLOCK) + bias[None]).reshape(ROWS, BLOCK)


def attend(q_rows, kaug_ref, vaug_ref, len_ref, low, high, qbd, top_ref, acc_ref):
    spread(qbd, q_rows)
    top_ref[...] = jnp.full(top_ref.shape, MASKED, f32)
    acc_ref[...] = jnp.zeros(acc_ref.shape, f32)
    first = low // 4 + 1

    def step(s, carry):
        late = s >= first
        u = late.astype(jnp.int32)
        tile = jnp.where(late, high, low)
        block = s - jnp.where(late, first, 0)
        scores = biased(nn(qbd[u], kaug_ref[block]), query_bias(u, tile, block, len_ref))
        old = top_ref[u]
        new = jnp.maximum(old, jnp.max(scores, axis=1, keepdims=True))
        probs = jnp.exp(scores - new)
        acc_ref[u] = acc_ref[u] * jnp.exp(old - new) + nt(probs.astype(bf16), vaug_ref[block])
        top_ref[u] = new
        return carry

    lax.fori_loop(0, STEPS, step, 0)
    attended, stats = [], []
    lane = iota((1, STAT), 1)
    for u in range(2):
        acc = acc_ref[u]
        total = acc[:, D : D + 1]
        attended.append(own_heads(acc[:, :D] / total))
        parts = three_parts(-(top_ref[u] + jnp.log(total)))
        stat = jnp.zeros((HALF, STAT), f32)
        for j in range(3):
            part = parts[j].astype(f32)
            for h in range(HEADS):
                stat = jnp.where(lane == 9 * j + h, part[h * HALF : (h + 1) * HALF], stat)
        stats.append(stat)
    att_rows = jnp.concatenate(attended, axis=0).astype(bf16)
    stat_rows = jnp.concatenate(stats, axis=0).astype(bf16)
    return nt(eye(D, D, bf16), att_rows).astype(bf16), nt(eye(STAT, STAT, bf16), stat_rows).astype(bf16)


def feed_forward(resid, attended, w_out, w_gate_up, w_down, gain):
    mid = resid + tn(w_out, attended)
    normal = (mid * norm_factor(mid) * gain).astype(bf16)
    gate_up = tn(w_gate_up, normal)
    gate = gate_up[:FF]
    hidden = (gate * jax.nn.sigmoid(gate) * gate_up[FF:]).astype(bf16)
    return mid, normal, gate_up, hidden, mid + tn(w_down, hidden)


def feed_back(grad, attended, mid, normal, gate_up, hidden, w_out, w_gate_up, w_down, gain, stat, pack_ref, first):
    d_out = grad.astype(bf16)
    at = put_tiles(pack_ref, first, nt(d_out, hidden))
    d_hidden = nn(w_down, d_out)
    gate, up = gate_up[:FF], gate_up[FF:]
    sig = jax.nn.sigmoid(gate)
    d_gate = d_hidden * up * (sig * (1.0 + gate * (1.0 - sig)))
    d_up = d_hidden * (gate * sig)
    d_gate_up = jnp.concatenate([d_gate, d_up], axis=0).astype(bf16)
    at = put_tiles(pack_ref, at, nt(normal, d_gate_up))
    d_mid, d_gain = norm_back(mid, gain, nn(w_gate_up, d_gate_up))
    grad = grad + d_mid
    d_branch = grad.astype(bf16)
    at = put_tiles(pack_ref, at, nt(attended, d_branch[:TILE]))
    zeros = jnp.zeros((TILE - 64, TILE), bf16)
    tail = nt(attended, jnp.concatenate([jnp.zeros((48, TILE), bf16), d_branch[TILE:], zeros], axis=0))
    d_att = nn(w_out, d_branch).astype(bf16)
    product = d_att.astype(f32) * attended.astype(f32)
    delta = -jnp.sum(product.reshape(HEADS, HEAD_DIM, TILE), axis=1)
    delta = jnp.concatenate([delta, jnp.zeros((16 - HEADS, TILE), f32)], axis=0)
    hi, lo, _ = three_parts(delta)
    row, col = iota((STAT, 16), 0), iota((STAT, 16), 1)
    place = [((row == 27 + 9 * j + col) & (col < HEADS)).astype(bf16) for j in range(2)]
    stat = stat.astype(f32) + nn(place[0], hi) + nn(place[1], lo)
    return grad, jnp.concatenate([d_att, stat.astype(bf16)], axis=0), tail, d_gain, at


def gain_column(gains_ref, which):
    return column(gains_ref[which : which + 1, :], D)


def first_kernel(
    len_ref, scale_ref, values_ref, lag_ref, w_lag_ref, w_qkv_ref, w_out_ref, w_gate_up_ref, w_down_ref, gains_ref, rope_ref,
    next_ref, next_resid_ref, kaug_ref, vaug_ref, qall_ref, lagged_ref, feats_ref, w_dense_ref, resid_ref, normal_a_ref,
    q_ref, k_ref, v_ref, att_ref, stat_ref, mid_ref, normal_b_ref, gate_up_ref, hidden_ref,
    series, toeplitz, extra, qbd, top_ref, acc_ref,
):
    chip, core, low, high = geometry()
    places = iota((TILES, TILE), 0) * TILE + iota((TILES, TILE), 1)
    own = doc_scale_at(places, len_ref, scale_ref)
    values = values_ref[:, 0, :] / own
    angle = values_ref[:, 1, :] * (2.0 * math.pi / 24.0)
    sine, cosine, level = jnp.sin(angle), jnp.cos(angle), jnp.log(own)
    series[0:8, :] = jnp.zeros((8, TILE), f32)
    series[8 : 8 + TILES, :] = values.astype(bf16).astype(f32)
    extra[...] = jnp.zeros(extra.shape, f32)
    for r in range(TILES):
        at = slice(r * TILE, (r + 1) * TILE)
        extra[0:1, at] = sine[r : r + 1]
        extra[1:2, at] = cosine[r : r + 1]
        extra[2:3, at] = level[r : r + 1]
    toeplitz[:, 0:MAXLAG] = jnp.zeros((TILE, MAXLAG), bf16)

    def shift(m, carry):
        window = jnp.concatenate([series[pl.ds(m + 7, 1), :], series[pl.ds(m + 8, 1), :]], axis=1)
        rolled = pltpu.roll(jnp.broadcast_to(window, (TILE, 2 * TILE)), 1, 1, stride=1, stride_axis=0)
        toeplitz[:, pl.ds(pl.multiple_of((m + 3) * TILE, TILE), TILE)] = rolled[:, TILE:].astype(bf16)
        return carry

    lax.fori_loop(0, TILES, shift, 0, unroll=4)

    rows = iota((FEATS, 1), 0)
    diagonal = iota((FEATS, LAGS), 0) == iota((FEATS, LAGS), 1)
    offsets = jnp.sum(jnp.where(diagonal, lag_ref[...].astype(f32), 0.0), axis=1, keepdims=True)
    offsets = jnp.where(rows < LAGS, offsets - 1.0, (rows - LAGS + MAXLAG).astype(f32))
    chosen = (iota((FEATS, LAGCOLS), 1).astype(f32) == offsets).astype(bf16)
    w_dense = tn(w_lag_ref[...], chosen).astype(bf16)
    w_dense_ref[...] = w_dense

    gain_a, gain_b = gain_column(gains_ref, 0), gain_column(gains_ref, 1)
    w_qkv = w_qkv_ref[0]
    lag_rows = iota((TILE, 1), 0) + 1
    for k in range(BLOCKS):
        place = iota((1, BLOCK), 1) + k * BLOCK
        start = doc_start(place, len_ref)
        resid = nn(w_dense[:, MAXLAG:], extra[:, k * BLOCK : (k + 1) * BLOCK].astype(bf16))
        for b in range(3):
            at = MAXLAG + k * BLOCK - b * TILE
            lagged = toeplitz[:, at : at + BLOCK]
            if k in (0, BLOCKS - 1):
                valid = place - (lag_rows + b * TILE) >= start
                lagged = jnp.where(valid, lagged.astype(f32), 0.0).astype(bf16)
            resid = resid + nn(w_dense[:, b * TILE : (b + 1) * TILE], lagged)
        normal = (resid * norm_factor(resid) * gain_a).astype(bf16)
        qkv_block(normal, w_qkv, rope_ref, k, kaug_ref, vaug_ref, qall_ref)

    place = own_places(low, high)
    start = doc_start(place, len_ref)
    lane = iota((1, TILE), 1)

    def tile_of(ref, tile):
        return ref[:, pl.ds(pl.multiple_of(tile * TILE, TILE), TILE)].astype(f32)

    for b in range(3):
        lagged = jnp.where(lane < HALF, tile_of(toeplitz, low + 3 - b), tile_of(toeplitz, high + 3 - b))
        valid = place - (lag_rows + b * TILE) >= start
        lagged_ref[b * TILE : (b + 1) * TILE, :] = jnp.where(valid, lagged, 0.0).astype(bf16)
    lagged_ref[MAXLAG:, :] = jnp.where(lane < HALF, tile_of(extra, low), tile_of(extra, high)).astype(bf16)
    lagged = lagged_ref[...]
    feats_ref[0:FEATS, :] = nn(chosen, lagged)
    feats_ref[FEATS:, :] = jnp.zeros((96 - FEATS, TILE), f32)
    resid = nn(w_dense, lagged)
    resid_ref[...] = resid
    normal_a_ref[...] = (resid * norm_factor(resid) * gain_a).astype(bf16)
    own_rows(qall_ref, kaug_ref, vaug_ref, low, high, q_ref, k_ref, v_ref)
    attended, stat_ref[...] = attend(q_ref[...].astype(f32), kaug_ref, vaug_ref, len_ref, low, high, qbd, top_ref, acc_ref)
    att_ref[...] = attended
    mid, normal_b, gate_up, hidden, resid = feed_forward(resid, attended, w_out_ref[0], w_gate_up_ref[0], w_down_ref[0], gain_b)
    mid_ref[...], normal_b_ref[...], gate_up_ref[...], hidden_ref[...] = mid, normal_b, gate_up, hidden
    next_resid_ref[...] = resid
    next_ref[...] = (resid * norm_factor(resid) * gain_column(gains_ref, 2)).astype(bf16)


def own_rows(qall_ref, kaug_ref, vaug_ref, low, high, q_ref, k_ref, v_ref):
    unit = eye(TILE, TILE, bf16)
    for source, target, fill in ((qall_ref, q_ref, 0.0), (kaug_ref, k_ref, 1.0), (vaug_ref, v_ref, 1.0)):
        target[:, :D] = nt(unit, own_tile(source, low, high)).astype(bf16)
        target[:, D:] = jnp.full((TILE, STAT), fill, bf16)


def natural_tiles(own_refs, other_refs, put):
    chip, core, _, _ = geometry()
    mine = (iota((1, TILE), 1) < HALF) == (core == 0)
    for k in range(4):
        for j in range(4):
            source = ((chip // 4) ^ k) * 4 + ((chip % 4) ^ j)
            own, other = own_refs[k][j].astype(f32), other_refs[k][j].astype(f32)
            put(source, jnp.where(mine, own, other).astype(bf16))
            put(TILES - 1 - source, jnp.where(mine, other, own).astype(bf16))


def second_kernel(*refs):
    own_refs, other_refs = refs[0:4], refs[4:8]
    (len_ref, resid_in_ref, cot_ref, w_qkv_ref, w_out_ref, w_gate_up_ref, w_down_ref, gains_ref, rope_ref,
     act_ref, kaug_ref, vaug_ref, qall_ref, q_ref, k_ref, v_ref, grad_ref, payload_ref, rows_ref, tail_ref, pack_ref,
     normal_all, qbd, top_ref, acc_ref) = refs[8:]
    chip, core, low, high = geometry()

    def put(tile, value):
        normal_all[tile // 4, :, pl.ds(pl.multiple_of((tile % 4) * TILE, TILE), TILE)] = value

    natural_tiles(own_refs, other_refs, put)
    w_qkv = w_qkv_ref[1]
    for k in range(BLOCKS):
        qkv_block(normal_all[k], w_qkv, rope_ref, k, kaug_ref, vaug_ref, qall_ref)
    own_rows(qall_ref, kaug_ref, vaug_ref, low, high, q_ref, k_ref, v_ref)
    attended, stat = attend(q_ref[...].astype(f32), kaug_ref, vaug_ref, len_ref, low, high, qbd, top_ref, acc_ref)
    gain = gain_column(gains_ref, 3)
    w_out, w_gate_up, w_down = w_out_ref[1], w_gate_up_ref[1], w_down_ref[1]
    mid, normal_b, gate_up, hidden, out = feed_forward(resid_in_ref[...], attended, w_out, w_gate_up, w_down, gain)
    act_ref[...] = nt(eye(TILE, TILE, f32), out, HIGH)
    grad = nt(eye(D, D, f32), cot_ref[...], HIGH)
    grad, payload, tail, d_gain, _ = feed_back(
        grad, attended, mid, normal_b, gate_up, hidden, w_out, w_gate_up, w_down, gain, stat, pack_ref, 0
    )
    grad_ref[...] = grad
    payload_ref[...] = payload
    rows_ref[...] = nt(eye(TILE, TILE, bf16), payload).astype(bf16)
    tail_ref[...] = jnp.where(iota((1, TILE), 1) == 99, d_gain, tail)


def query_back_kernel(len_ref, q_ref, rows_ref, kaug_ref, vaug_ref, dq_ref, qbd, dbd, acc_ref):
    chip, core, low, high = geometry()
    rows = rows_ref[...].astype(f32)
    spread(qbd, jnp.concatenate([q_ref[:, :D].astype(f32), rows[:, D:]], axis=1), LROW, LROW + 9, LROW + 18)
    spread(dbd, rows, DROW, DROW + 9)
    acc_ref[...] = jnp.zeros(acc_ref.shape, f32)
    first = low // 4 + 1

    def step(s, carry):
        late = s >= first
        u = late.astype(jnp.int32)
        tile = jnp.where(late, high, low)
        block = s - jnp.where(late, first, 0)
        scores = biased(nn(qbd[u], kaug_ref[block]), query_bias(u, tile, block, len_ref))
        d_scores = jnp.exp(scores) * nn(dbd[u], vaug_ref[block])
        acc_ref[u] = acc_ref[u] + nt(d_scores.astype(bf16), kaug_ref[block])
        return carry

    lax.fori_loop(0, STEPS, step, 0)
    for u in range(2):
        dq_ref[u * HALF : (u + 1) * HALF, :] = own_heads(acc_ref[u]) * HEAD_DIM**-0.5


def key_back(own_refs, other_refs, len_ref, qall_ref, k_ref, v_ref, dq_ref, grad, resid, normal, w_qkv, gain, rope_ref,
             qaug, daug, kbd, vbd, dk_ref, dv_ref):
    chip, core, low, high = geometry()

    def put(tile, value):
        at = pl.ds(pl.multiple_of((tile % 4) * TILE, TILE), TILE)
        daug[tile // 4, :, at] = value
        qaug[tile // 4, D:AUG, at] = value[D:]

    natural_tiles(own_refs, other_refs, put)
    qaug[:, 0:D, :] = qall_ref[...]
    spread(kbd, k_ref[...].astype(f32), LROW, LROW + 9, LROW + 18)
    spread(vbd, v_ref[...].astype(f32), DROW, DROW + 9)
    dk_ref[...] = jnp.zeros(dk_ref.shape, f32)
    dv_ref[...] = jnp.zeros(dv_ref.shape, f32)
    first = BLOCKS - low // 4

    def step(s, carry):
        late = s >= first
        u = late.astype(jnp.int32)
        tile = jnp.where(late, high, low)
        block = tile // 4 + s - jnp.where(late, first, 0)
        probs = jnp.exp(biased(nn(kbd[u], qaug[block]), key_bias(u, tile, block, len_ref)))
        d_scores = probs * nn(vbd[u], daug[block])
        dv_ref[u] = dv_ref[u] + nt(probs.astype(bf16), daug[block])
        dk_ref[u] = dk_ref[u] + nt(d_scores.astype(bf16), qaug[block])
        return carry

    lax.fori_loop(0, STEPS, step, 0)
    unit = eye(D, D, f32)
    d_query = nt(unit, dq_ref[...], HIGH)
    d_key = nt(unit, jnp.concatenate([own_heads(dk_ref[0]), own_heads(dk_ref[1])], axis=0), HIGH)
    d_value = nt(unit, jnp.concatenate([own_heads(dv_ref[0]), own_heads(dv_ref[1])], axis=0), HIGH)
    lane = iota((1, TILE), 1)

    def rope_of(tile):
        return rope_ref[:, pl.ds(pl.multiple_of(tile * TILE, TILE), TILE)]

    rope = jnp.where(lane < HALF, rope_of(low), rope_of(high))
    cosine, sine = rope[0:8], -rope[8:16]
    d_mixed = jnp.concatenate([rotate(d_query, cosine, sine), rotate(d_key, cosine, sine), d_value], axis=0).astype(bf16)
    d_in, d_gain = norm_back(resid, gain, nn(w_qkv, d_mixed))
    head = nt(normal, d_mixed[:MAXLAG])
    tail = nt(normal, jnp.concatenate([d_mixed[MAXLAG:], jnp.zeros((TILE - 48, TILE), bf16)], axis=0))
    return grad + d_in, head, tail, d_gain


def third_kernel(*refs):
    own_refs, other_refs = refs[0:4], refs[4:8]
    (len_ref, qall_ref, k_ref, v_ref, dq_ref, grad_in_ref, resid_ref, normal_a_ref, tail_in_ref, w_qkv_ref, w_out_ref, w_gate_up_ref,
     w_down_ref, gains_ref, rope_ref, att_ref, stat_ref, mid_ref, normal_b_ref, gate_up_ref, hidden_ref,
     grad_ref, payload_ref, rows_ref, tail_ref, tail1_ref, pack_ref,
     qaug, daug, kbd, vbd, dk_ref, dv_ref) = refs[8:]
    grad, head, tail1, d_gain = key_back(
        own_refs, other_refs, len_ref, qall_ref, k_ref, v_ref, dq_ref, grad_in_ref[...], resid_ref[...], normal_a_ref[...],
        w_qkv_ref[1], gain_column(gains_ref, 2), rope_ref, qaug, daug, kbd, vbd, dk_ref, dv_ref,
    )
    at = put_tiles(pack_ref, 0, head)
    lane = iota((1, TILE), 1)
    tail1 = tail1 + tail_in_ref[...]
    tail1 = jnp.where(lane == 98, d_gain, tail1)
    grad, payload, tail, d_gain, _ = feed_back(
        grad, att_ref[...], mid_ref[...], normal_b_ref[...], gate_up_ref[...], hidden_ref[...], w_out_ref[0], w_gate_up_ref[0],
        w_down_ref[0], gain_column(gains_ref, 1), stat_ref[...], pack_ref, at,
    )
    grad_ref[...] = grad
    payload_ref[...] = payload
    rows_ref[...] = nt(eye(TILE, TILE, bf16), payload).astype(bf16)
    tail_ref[...] = tail
    tail1_ref[...] = jnp.where(lane == 97, d_gain, tail1)


def last_kernel(*refs):
    own_refs, other_refs = refs[0:4], refs[4:8]
    (len_ref, scale_ref, ids_ref, qall_ref, k_ref, v_ref, dq_ref, grad_in_ref, resid_ref, normal_a_ref, tail_in_ref, tail1_ref, pack2_ref,
     pack3_ref, w_qkv_ref, gains_ref, rope_ref, w_dense_ref, feats_ref,
     out_ref, qaug, daug, kbd, vbd, dk_ref, dv_ref, raw_ref) = refs[8:]
    chip, core, low, high = geometry()
    d_first, head, tail0, d_gain = key_back(
        own_refs, other_refs, len_ref, qall_ref, k_ref, v_ref, dq_ref, grad_in_ref[...], resid_ref[...], normal_a_ref[...],
        w_qkv_ref[0], gain_column(gains_ref, 0), rope_ref, qaug, daug, kbd, vbd, dk_ref, dv_ref,
    )
    d_first = d_first.astype(bf16)
    feats = feats_ref[...].astype(bf16)
    empty = jnp.zeros((64, TILE), bf16)
    tail0 = tail0 + tail_in_ref[...] + nt(d_first, jnp.concatenate([empty, feats[:64]], axis=0))
    tail1 = tail1_ref[...] + nt(d_first, jnp.concatenate([empty, feats[64:], empty[:32]], axis=0))
    lane, row = iota((1, TILE), 1), iota((D, 1), 0)
    tail1 = jnp.where(lane == 96, d_gain, tail1)
    sums, counts = jnp.zeros((D, 1), f32), jnp.zeros((D, 1), f32)
    owner = (lax.axis_index("tm") == 0).astype(f32)
    for d in range(DOCS):
        hit = jnp.where(row == ids_ref[d], owner, 0.0)
        sums, counts = sums + hit * scale_ref[d], counts + hit
    high_part = sums.astype(bf16).astype(f32)
    tail1 = jnp.where(lane == 100, high_part, tail1)
    tail1 = jnp.where(lane == 101, sums - high_part, tail1)
    tail1 = jnp.where(lane == 102, counts, tail1)

    place = own_places(low, high)
    start = doc_start(place, len_ref)
    own = doc_scale_at(place, len_ref, scale_ref)
    flip = (iota((TILE, TILE), 0) + iota((TILE, TILE), 1) == TILE - 1).astype(bf16)
    raw_ref[...] = jnp.zeros(raw_ref.shape, f32)
    lags = TILE - iota((TILE, 1), 0)
    for b in range(3):
        weights = nn(w_dense_ref[:, b * TILE : (b + 1) * TILE], flip).astype(bf16)
        d_lagged = tn(weights, d_first)
        valid = place - (lags + b * TILE) >= start
        d_lagged = jnp.where(valid, d_lagged, 0.0) / own
        for u in range(2):
            half = jnp.where((lane < HALF) == (u == 0), d_lagged, 0.0)
            wide = jnp.concatenate([jnp.zeros((TILE, TILE), f32), half], axis=1)
            rolled = pltpu.roll(wide, TILE, 1, stride=1, stride_axis=0)
            total = jnp.sum(rolled, axis=0, keepdims=True)
            tile = (low if u == 0 else high) - b + 8
            raw_ref[pl.ds(tile, 1), :] = raw_ref[pl.ds(tile, 1), :] + total[:, TILE:]
            raw_ref[pl.ds(tile - 1, 1), :] = raw_ref[pl.ds(tile - 1, 1), :] + total[:, :TILE]

    out_ref[:, 2] = jnp.zeros((128, 16, TILE), bf16)
    group = lax.axis_index("series") * TILES
    for r in range(TILES):
        line = jnp.broadcast_to(raw_ref[8 + r : 9 + r, :], (16, TILE))
        out_ref[group + r, 2] = jnp.where(iota((16, 1), 0) == 0, line, 0.0).astype(bf16)
    for t in range(90):
        out_ref[t // 2, t % 2] = pack2_ref[t]
    for t in range(117):
        out_ref[(t + 90) // 2, t % 2] = pack3_ref[t]
    at = 207
    for part in (head, tail0, tail1):
        for c in range(part.shape[1] // TILE):
            for r in range(9):
                out_ref[at // 2, at % 2] = part[16 * r : 16 * (r + 1), c * TILE : (c + 1) * TILE].astype(bf16)
                at += 1
    for t in range(at, 256):
        out_ref[t // 2, t % 2] = jnp.zeros((16, TILE), bf16)


def sum_kernel(in_ref, out_ref, raw_ref):
    total = jnp.zeros((3, 16, TILE), f32)
    total = lax.fori_loop(0, 16, lambda i, t: t + jnp.sum(in_ref[pl.ds(i * 8, 8)].astype(f32), axis=0), total)
    out_ref[...] = total[:2].astype(bf16)
    raw_ref[...] = total[2, 0:1]


def unpack_kernel(in_ref, lag_ref, qkv_ref, out_ref, gate_up_ref, down_ref, gains_ref, scale_ref):
    def tile(t):
        return in_ref[t // 2, t % 2]

    def columns(first, count):
        return [jnp.concatenate([tile(first + 9 * c + r) for r in range(9)], axis=0) for c in range(count)]

    layers = ((207, 234, 117), (90, 243, 0))
    unit = eye(TILE, TILE, bf16)
    tails = []
    for layer, (at_qkv, at_tail, at_rest) in enumerate(layers):
        for c, part in enumerate(columns(at_qkv, 3)):
            qkv_ref[layer, :, c * TILE : (c + 1) * TILE] = part.astype(f32)
        tail = columns(at_tail, 1)[0]
        tails.append(tail)
        qkv_ref[layer, :, MAXLAG:] = tail[:, :48].astype(f32)
        for c, part in enumerate(columns(at_rest, 3)):
            down_ref[layer, c * TILE : (c + 1) * TILE, :] = nt(unit, part)
        for c, part in enumerate(columns(at_rest + 27, 6)):
            gate_up_ref[layer, :, c * TILE : (c + 1) * TILE] = part.astype(f32)
        out_ref[layer, :, :TILE] = columns(at_rest + 81, 1)[0].astype(f32)
        out_ref[layer, :, TILE:] = tail[:, 48:64].astype(f32)
    row, lane = iota((96, TILE), 0), iota((96, TILE), 1)
    pick0 = ((lane == row + 64) & (row < 64)).astype(bf16)
    pick1 = ((lane == row) & (row >= 64) & (row < FEATS)).astype(bf16)
    lag = nt(pick0, tails[0]) + nt(pick1, tails[1])
    lag_ref[...] = lag[:FEATS]
    rest = nt((iota((8, TILE), 1) == iota((8, TILE), 0) + 96).astype(bf16), tails[1])
    gains_ref[...] = rest[:4]
    scale_ref[...] = (rest[4:5] + rest[5:6]) / rest[6:7]


def shape(*dims, dtype=f32):
    return jax.ShapeDtypeStruct(dims, dtype)


def call(kernel, smem, operands, outs, scratch):
    count = len(operands)
    specs = [pl.BlockSpec(memory_space=pltpu.SMEM if n in smem else pltpu.VMEM) for n in range(count)]
    return pl.pallas_call(
        kernel,
        out_shape=outs,
        in_specs=specs,
        out_specs=jax.tree.map(lambda _: pl.BlockSpec(memory_space=pltpu.VMEM), outs),
        scratch_shapes=scratch,
        compiler_params=pltpu.CompilerParams(vmem_limit_bytes=VMEM),
    )(*operands)


def pair_permute(x, bit):
    return lax.ppermute(x, "tm", [(i, i ^ bit) for i in range(32)])


def gather(block):
    near = jnp.stack([block] + [pair_permute(block, 2 * k) for k in range(1, 4)])
    own = [near] + [pair_permute(near, 8 * k) for k in range(1, 4)]
    return own + [pair_permute(piece, 1) for piece in own]


def to_halves(n, which):
    if n < 16:
        return 2 * n + which
    return 63 - 2 * n - which


def rope_table():
    freqs = 10000.0 ** (-np.arange(8, dtype=np.float64) / 8)
    angle = np.arange(LEN, dtype=np.float64)[None, :] * freqs[:, None]
    return np.concatenate([np.cos(angle), np.sin(angle)], axis=0).astype(np.float32)


def body(
    raw_values, hours, doc_lengths, doc_scale, dataset_ids, lag_offsets, w_lag, w_qkv, w_out, w_gate_up, w_down, gains, cotangent
):
    lengths, scales, ids = doc_lengths.reshape(DOCS), doc_scale.reshape(DOCS), dataset_ids.reshape(DOCS)
    gains4 = gains.reshape(2 * LAYERS, D)
    rope = jnp.asarray(rope_table())
    both = jnp.concatenate([raw_values, hours.astype(f32)], axis=0)
    values = lax.all_to_all(jnp.broadcast_to(both[None], (32, 2, TILE)), "tm", 0, 0)
    cot = [
        lax.ppermute(cotangent[0, w * HALF : (w + 1) * HALF], "tm", [(n, to_halves(n, w)) for n in range(32)]) for w in range(2)
    ]
    cot = jnp.concatenate(cot, axis=0)
    wide = [shape(BLOCKS, AUG, BLOCK, dtype=bf16), shape(BLOCKS, AUG, BLOCK, dtype=bf16), shape(BLOCKS, D, BLOCK, dtype=bf16)]
    rows = [shape(TILE, AUG, dtype=bf16)] * 3
    narrow, narrow_low = shape(D, TILE), shape(D, TILE, dtype=bf16)
    payload_shape = shape(AUG, TILE, dtype=bf16)
    bd = pltpu.VMEM((2, ROWS, AUG), bf16)
    acc = pltpu.VMEM((2, ROWS, AUG), f32)
    top = pltpu.VMEM((2, ROWS, 1), f32)
    aug = pltpu.VMEM((BLOCKS, AUG, BLOCK), bf16)

    (next1, resid1, kaug0, vaug0, qall0, lagged, feats, w_dense, resid0, normal_a0, q0, k0, v0, att0, stat0, mid0, normal_b0,
     gate_up0, hidden0) = call(
        first_kernel, (0, 1),
        (lengths, scales, values, lag_offsets.reshape(1, LAGS), w_lag, w_qkv, w_out, w_gate_up, w_down, gains4, rope),
        [narrow_low, narrow] + wide
        + [shape(LAGCOLS, TILE, dtype=bf16), shape(96, TILE), shape(D, LAGCOLS, dtype=bf16), narrow, narrow_low]
        + rows
        + [narrow_low, shape(STAT, TILE, dtype=bf16), narrow, narrow_low, shape(2 * FF, TILE), shape(FF, TILE, dtype=bf16)],
        [pltpu.VMEM((8 + TILES, TILE), f32), pltpu.VMEM((TILE, MAXLAG + LEN), bf16), pltpu.VMEM((16, LEN), f32), bd, top, acc],
    )

    act, kaug1, vaug1, qall1, q1, k1, v1, grad, payload, payload_rows, tail1, pack2 = call(
        second_kernel, (8,),
        (*gather(next1), lengths, resid1, cot, w_qkv, w_out, w_gate_up, w_down, gains4, rope),
        [shape(TILE, D)] + wide + rows
        + [narrow, payload_shape, shape(TILE, AUG, dtype=bf16), narrow, shape(90, 16, TILE, dtype=bf16)],
        [pltpu.VMEM((BLOCKS, D, BLOCK), bf16), bd, top, acc],
    )
    act = [
        lax.ppermute(act[w * HALF : (w + 1) * HALF], "tm", [(to_halves(n, w), n) for n in range(32)]) for w in range(2)
    ]

    def query_back(q, payload_rows, kaug, vaug):
        return call(query_back_kernel, (0,), (lengths, q, payload_rows, kaug, vaug), shape(TILE, D), [bd, bd, acc])

    pieces = gather(payload)
    dq = query_back(q1, payload_rows, kaug1, vaug1)
    grad, payload, payload_rows, tail0, tail1, pack3 = call(
        third_kernel, (8,),
        (*pieces, lengths, qall1, k1, v1, dq, grad, resid1, next1, tail1, w_qkv, w_out, w_gate_up, w_down, gains4, rope,
         att0, stat0, mid0, normal_b0, gate_up0, hidden0),
        [narrow, payload_shape, shape(TILE, AUG, dtype=bf16), narrow, narrow, shape(117, 16, TILE, dtype=bf16)],
        [aug, aug, bd, bd, acc, acc],
    )
    pieces = gather(payload)
    dq = query_back(q0, payload_rows, kaug0, vaug0)
    packed = call(
        last_kernel, (8, 9, 10),
        (*pieces, lengths, scales, ids, qall0, k0, v0, dq, grad, resid0, normal_a0, tail0, tail1, pack2, pack3, w_qkv, gains4, rope,
         w_dense, feats),
        shape(128, 3, 16, TILE, dtype=bf16),
        [aug, aug, bd, bd, acc, acc, pltpu.VMEM((8 + TILES, TILE), f32)],
    )
    parts = lax.all_to_all(packed, ("series", "tm"), 0, 0)
    share, raw_grad = call(sum_kernel, (), (parts,), [shape(2, 16, TILE, dtype=bf16), shape(1, TILE)], [])
    shares = lax.all_to_all(jnp.broadcast_to(share[None], (128, 2, 16, TILE)), ("series", "tm"), 0, 0)
    g_lag, g_qkv, g_out, g_gate_up, g_down, g_gains, scale = call(
        unpack_kernel, (), (shares,),
        [shape(FEATS, D), shape(LAYERS, D, 3 * D), shape(LAYERS, D, D), shape(LAYERS, D, 2 * FF), shape(LAYERS, FF, D),
         shape(2 * LAYERS, D), shape(1, D)],
        [],
    )
    act = jnp.concatenate(act, axis=0)
    return (
        act[None], raw_grad, scale[0, :DATASETS], g_lag, g_qkv, g_out, g_gate_up, g_down, g_gains.reshape(LAYERS, 2, D),
    )


def solution(mesh):
    placed = (
        P("series", "tm"),
        P("series", "tm"),
        P("series", None),
        P("series", None),
        P("series", None, None),
        P(),
        P(),
        P(),
        P(),
        P(),
        P(),
        P(),
        P("series", "tm", None),
    )
    return jax.shard_map(
        body,
        mesh=mesh,
        in_specs=placed,
        out_specs=(P("series", "tm", None), P("series", "tm"), P(), P(), P(), P(), P(), P(), P()),
        check_vma=False,
    )
```

time: 647 us -> 240 us (0.37); the launches traced: 637 us -> 239 us
  matrix products: 207 us -> 0 us
  other arithmetic: 117 us -> 4.46 us
  Pallas kernels: 0 us -> 87 us
  blocking collectives: 118 us -> 32.2 us
  waiting for transfers between devices: 85.9 us -> 26.5 us
  local copies, waits for them, and re-layouts: 76.3 us -> 18.5 us
  starting transfers between devices: 16.7 us -> 69.6 us
  between operations: 15.9 us -> 1.06 us
    dot_general x43 -> x0, matrix products: 207 us -> none  [the longest x4 47 us: scores_of(): jnp.einsum('thd,jhd->htj', queries, keys, preferred_element_type=jnp.floa...]
    pallas_call x0 -> x8, Pallas kernels: none -> 87 us  [call(): pl.pallas_call(kernel, out_shape=outs, in_specs=specs, out_specs=jax.tree...]
    all_gather x4 -> x0, waiting for transfers between devices: 85.8 us -> none  [side_by_side(): out, at, done = (lax.all_gather(both, axis, axis=dim, tiled=True), 0, [])]
    scatter-add x1 -> x0, other arithmetic: 75 us -> none  [lag_features(): lagged = jnp.take(extended, index)]
    psum x1 -> x0, blocking collectives: 69.9 us -> none  [body(): lax.psum((g_lag, stacked[0], stacked[1], stacked[2], stacked[3], stacked[...]
    gather x3 -> x0, local copies, waits for them, and re-layouts: 63.3 us -> none  [lag_features(): lagged = jnp.take(extended, index)]
    all_gather x2 -> x0, blocking collectives: 47.6 us -> none  [side_by_side(): out, at, done = (lax.all_gather(both, axis, axis=dim, tiled=True), 0, [])]
    ppermute x6 -> x34, starting transfers between devices: 16 us -> 55.4 us  [the longest x30 42.1 us: pair_permute(): return lax.ppermute(x, 'tm', [(i, i ^ bit) for i in range(32)])]
  transfers between devices with their start and end apart: 11 -> 36, of which waited for: 2 -> 14; matrix products, arithmetic and copies ran while one was open for 24% -> 3% of each run, Pallas kernels for 0% -> 8%
where the time goes in v1:
time: 240 us; the launch traced here: 239 us
  Pallas kernels  87 us (36%)
  starting transfers between devices  69.6 us (29%)
  blocking collectives  32.2 us (13%)
  waiting for transfers between devices  26.5 us (11%)
  local copies, waits for them, and re-layouts  18.5 us (8%)
  other arithmetic  4.46 us (2%)
    pallas_call x8, Pallas kernels, call(): pl.pallas_call(kernel, out_shape=outs, in_specs=specs, out_specs=jax.tree...  87 us
    ppermute x30, starting transfers between devices, pair_permute(): return lax.ppermute(x, 'tm', [(i, i ^ bit) for i in range(32)])  42.1 us
    all_to_all x1, blocking collectives, body(): parts = lax.all_to_all(packed, ('series', 'tm'), 0, 0)  32.2 us
    ppermute x30, waiting for transfers between devices, pair_permute(): return lax.ppermute(x, 'tm', [(i, i ^ bit) for i in range(32)])  12.7 us
    unnamed x63, local copies, waits for them, and re-layouts  12.2 us
    all_to_all x1, starting transfers between devices, body(): lax.all_to_all(jnp.broadcast_to(both[None], (32, 2, TILE)), 'tm', 0, 0)  9.6 us
    ppermute x2, waiting for transfers between devices, body(): lax.ppermute(act[w * HALF:(w + 1) * HALF], 'tm', [(to_halves(n, w), n) fo...  8.33 us
    ppermute x2, starting transfers between devices, body(): lax.ppermute(act[w * HALF:(w + 1) * HALF], 'tm', [(to_halves(n, w), n) fo...  7.7 us
  transfers between devices with their start and end apart: 36, of which 14 were waited for; matrix products, arithmetic and copies ran while one was open for 3% of the time, Pallas kernels for 8%

profile of v1, /device:TPU:1, one launch (start us, length us, event | category | flops | bytes accessed | tf_op | source)
XLA Modules:
  0.0 239.4 jit_solution(14206435449780808658)
XLA Ops:
  2.6 9.6 %all-to-all-start = ((f32[32,2,128]{2,1,0:T(2,128)}), f32[32,2,128]{2,1,0:T(2,128)S(1)}, u32[]{:S(2)}, u32[]{:S(2)}) async-start(f32[32,2,128]{2,1,0:T(2,128)} %broadcast_in_dim.6), calls=%async_computation | async-start | bytes 65536 | tf_op jit(solution)/shard_map/all_to_all | solution.py:657
  15.0 1.9 copy.24.w_down_ref.refs_14_.refs_20_
  16.9 2.6 %all-to-all-done.values_ref = f32[32,2,128]{2,1,0:T(2,128)S(1)} async-done(((f32[32,2,128]{2,1,0:T(2,128)}), f32[32,2,128]{2,1,0:T(2,128)S(1)}, u32[]{:S(2)}, u32[]{:S(2)}) %all-to-all-start) | async-done | bytes 32800 | tf_op jit(solution)/shard_map/all_to_all | solution.py:657
  20.1 19.9 %shard_map.205 = (bf16[144,128]{1,0:T(8,128)(2,1)}, f32[144,128]{1,0:T(8,128)}, bf16[8,192,512]{2,1,0:T(8,128)(2,1)}, bf16[8,192,512]{2,1,0:T(8,128)(2,1)}, bf16...) custom-call(s32[7]{0:T(128)} %bitcast.36, ...), custom_call_target="tpu_custom_call" | custom-call | tf_op jit(solution)/shard_map/pallas_call | solution.py:618
  51.4 4.2 %collective-permute-start.10 = (f32[64,144]{1,0:T(8,128)S(1)}, f32[64,144]{1,0:T(8,128)S(1)}, u32[]{:S(2)}, u32[]{:S(2)}) collective-permute-start(f32[64,144]{1,0:T(8,128)S(1)} %bitcast.23), channel_id=1, source_target_pairs={{0,0},{1,2},{2,4},{3,6},{4,8},{5,10},{6,12},{7,14},{8,16},{9,18},{... | collective-permute-start | bytes 110600 | tf_op jit(solution)/shard_map/ppermute | solution.py:659
  55.6 4.0 %collective-permute-start.6 = (bf16[4,144,128]{2,1,0:T(8,128)(2,1)S(1)}, bf16[4,144,128]{2,1,0:T(8,128)(2,1)S(1)}, u32[]{:S(2)}, u32[]{:S(2)}) collective-permute-start(bf16[4,144,128]{2,1,0:T(8,128)(2,1)S(1)} %pad_maximum_fusion.2.refs_0_), channel_id=1, source_target_pairs={{0,1},{1,0},{2,3},{3,2},{4,5},{5,4},{6,7},{7,6},{8,9},{9,8},{10,11... | collective-permute-start | bytes 442376 | tf_op jit(solution)/shard_map/ppermute | solution.py:629
  62.4 16.6 %shard_map.206 = (f32[128,144]{1,0:T(8,128)}, bf16[8,192,512]{2,1,0:T(8,128)(2,1)}, bf16[8,192,512]{2,1,0:T(8,128)(2,1)}, bf16[8,144,512]{2,1,0:T(8,128)(2,1)}, ...) custom-call(bf16[4,144,128]{2,1,0:T(8,128)(2,1)} %copy-done.3, ...), custom_call_target="tpu_custom_call" | custom-call | tf_op jit(solution)/shard_map/pallas_call | solution.py:618
  80.3 2.6 %collective-permute-start.15 = (bf16[192,128]{1,0:T(8,128)(2,1)}, bf16[192,128]{1,0:T(8,128)(2,1)S(1)}, u32[]{:S(2)}, u32[]{:S(2)}) collective-permute-start(bf16[192,128]{1,0:T(8,128)(2,1)} %get-tuple-element.57), channel_id=1, source_target_pairs={{0,4},{1,5},{2,6},{3,7},{4,0},{5,1},{6,2},{7,3},{8,12},{9,13},{10,... | collective-permute-start | bytes 147464 | tf_op jit(solution)/shard_map/ppermute | solution.py:629
  86.9 2.4 collective-permute-start.19
  90.2 4.3 %collective-permute-start.20 = (bf16[4,192,128]{2,1,0:T(8,128)(2,1)S(1)}, bf16[4,192,128]{2,1,0:T(8,128)(2,1)S(1)}, u32[]{:S(2)}, u32[]{:S(2)}) collective-permute-start(bf16[4,192,128]{2,1,0:T(8,128)(2,1)S(1)} %pad_maximum_fusion.refs_0_), channel_id=1, source_target_pairs={{0,1},{1,0},{2,3},{3,2},{4,5},{5,4},{6,7},{7,6},{8,9},{9,8},{10,11... | collective-permute-start | bytes 589832 | tf_op jit(solution)/shard_map/ppermute | solution.py:629
  94.5 4.3 %collective-permute-start.23 = (bf16[4,192,128]{2,1,0:T(8,128)(2,1)S(1)}, bf16[4,192,128]{2,1,0:T(8,128)(2,1)S(1)}, u32[]{:S(2)}, u32[]{:S(2)}) collective-permute-start(bf16[4,192,128]{2,1,0:T(8,128)(2,1)S(1)} %collective-permute-done.19.refs_3_), channel_id=1, source_target_pairs={{0,1},{1,0},{2,3},{3,2},{4,5},{5,4},{6,7},{7,6},{8,9},{9,8},{10,11... | collective-permute-start | bytes 589832 | tf_op jit(solution)/shard_map/ppermute | solution.py:629
  98.8 1.9 collective-permute-start.22
  100.8 9.5 %shard_map.207.refs_12_ = f32[128,144]{1,0:T(8,128)} custom-call(s32[7]{0:T(128)} %bitcast.38, bf16[128,192]{1,0:T(8,128)(2,1)} %get-tuple-element.61.q_ref, bf16[128,192]{1,0:T(8,128)(2,1)} %get-tuple-element.62.rows_ref, bf16[8,192,512]{2,1,0:T(8,128)(2,1)} %get-tuple-element.63.kaug_ref, bf16[8,192,512]{2,1,0:T(8,128)(2,1)} %get-tuple-element.64.vaug_ref), custom_call_target="tpu_custom_call" | custom-call | tf_op jit(solution)/shard_map/pallas_call | solution.py:618
  111.3 13.1 %shard_map.208 = (f32[144,128]{1,0:T(8,128)}, bf16[192,128]{1,0:T(8,128)(2,1)}, bf16[128,192]{1,0:T(8,128)(2,1)}, f32[144,128]{1,0:T(8,128)}, f32[144,128]{1,0:T(8,128)}, /*index=5*/bf16[117,16,128]{2,1,0:T(8,128)(2,1)}) custom-call(bf16[4,192,128]{2,1,0:T(8,128)(2,1)} %copy-done.1, bf16[4,192,128]{2,1,0:T(8,128)(2,1)} %copy-done.8, ...), custom_call_target="tpu_custom_call" | custom-call | tf_op jit(solution)/shard_map/pallas_call | solution.py:618
  124.3 1.9 collective-permute-start.26
  128.8 2.2 collective-permute-done.25
  131.9 2.3 collective-permute-start.29
  135.2 2.6 %collective-permute-start.30 = (bf16[4,192,128]{2,1,0:T(8,128)(2,1)S(1)}, bf16[4,192,128]{2,1,0:T(8,128)(2,1)S(1)}, u32[]{:S(2)}, u32[]{:S(2)}) collective-permute-start(bf16[4,192,128]{2,1,0:T(8,128)(2,1)S(1)} %pad_maximum_fusion.1.refs_0_), channel_id=1, source_target_pairs={{0,1},{1,0},{2,3},{3,2},{4,5},{5,4},{6,7},{7,6},{8,9},{9,8},{10,11... | collective-permute-start | bytes 589832 | tf_op jit(solution)/shard_map/ppermute | solution.py:629
  137.8 3.9 %collective-permute-done.29.refs_3_ = bf16[4,192,128]{2,1,0:T(8,128)(2,1)S(1)} collective-permute-done((bf16[4,192,128]{2,1,0:T(8,128)(2,1)S(1)}, bf16[4,192,128]{2,1,0:T(8,128)(2,1)S(1)}, u32[]{:S(2)}, u32[]{:S(2)}) %collective-permute-start.29) | collective-permute-done | bytes 196640 | tf_op jit(solution)/shard_map/ppermute | solution.py:629
  141.7 2.4 collective-permute-start.33
  145.3 9.5 %shard_map.209.refs_14_ = f32[128,144]{1,0:T(8,128)} custom-call(s32[7]{0:T(128)} %bitcast.40, bf16[128,192]{1,0:T(8,128)(2,1)} %get-tuple-element.77.q_ref, bf16[128,192]{1,0:T(8,128)(2,1)} %get-tuple-element.78.rows_ref, bf16[8,192,512]{2,1,0:T(8,128)(2,1)} %get-tuple-element.79.kaug_ref, bf16[8,192,512]{2,1,0:T(8,128)(2,1)} %get-tuple-element.80.vaug_ref), custom_call_target="tpu_custom_call" | custom-call | tf_op jit(solution)/shard_map/pallas_call | solution.py:618
  155.9 13.0 %shard_map.210 = bf16[128,3,16,128]{3,2,1,0:T(8,128)(2,1)} custom-call(bf16[4,192,128]{2,1,0:T(8,128)(2,1)} %copy-done.2, bf16[4,192,128]{2,1,0:T(8,128)(2,1)} %copy-done.11, bf16[4,192,128]{2,1,0:T(8,128)(2,1)} %copy-done.9, bf16[4,192,128]{2,1,0:T(8,128)(2,1)} %copy-done.7, bf16[4,192,128]{2,1,0:T(8,128)(2,1)} %copy-done.12, ...), custom_call_target="tpu_custom_call" | custom-call | tf_op jit(solution)/shard_map/pallas_call | solution.py:618
  168.9 32.2 %all_to_all.15.in_ref = bf16[128,3,16,128]{3,2,1,0:T(8,128)(2,1)} all-to-all(bf16[128,3,16,128]{3,2,1,0:T(8,128)(2,1)} %shard_map.210), channel_id=1, replica_groups=mesh['series'=4,'tm'=32] {'series','tm'}, dimensions={0} | all-to-all | bytes 3145728 | tf_op jit(solution)/shard_map/all_to_all | solution.py:714
  201.1 2.3 shard_map.211
  203.4 1.9 broadcast_in_dim.8
  205.3 4.6 %all-to-all-start.2 = ((bf16[128,2,16,128]{3,2,1,0:T(8,128)(2,1)}), bf16[128,2,16,128]{3,2,1,0:T(8,128)(2,1)S(1)}, u32[]{:S(2)}, u32[]{:S(2)}) async-start(bf16[128,2,16,128]{3,2,1,0:T(8,128)(2,1)} %broadcast_in_dim.8), calls=%async_computation.2 | async-start | bytes 2097152 | tf_op jit(solution)/shard_map/all_to_all | solution.py:716
  209.9 7.6 %collective-permute-start.12 = (f32[64,144]{1,0:T(8,128)S(1)}, f32[64,144]{1,0:T(8,128)S(1)}, u32[]{:S(2)}, u32[]{:S(2)}) collective-permute-start(f32[64,144]{1,0:T(8,128)S(1)} %get-tuple-element.108), channel_id=1, source_target_pairs={{0,0},{2,1},{4,2},{6,3},{8,4},{10,5},{12,6},{14,7},{16,8},{18,9},{... | collective-permute-start | bytes 110600 | tf_op jit(solution)/shard_map/ppermute | solution.py:690
  217.6 7.1 %collective-permute-done.12 = f32[64,144]{1,0:T(8,128)S(1)} collective-permute-done((f32[64,144]{1,0:T(8,128)S(1)}, f32[64,144]{1,0:T(8,128)S(1)}, u32[]{:S(2)}, u32[]{:S(2)}) %collective-permute-start.12) | collective-permute-done | bytes 36896 | tf_op jit(solution)/shard_map/ppermute | solution.py:690
  226.7 2.4 all-to-all-done.2.in_ref
  230.1 3.0 %shard_map.212 = (f32[87,144]{1,0:T(8,128)}, f32[2,144,432]{2,1,0:T(8,128)}, f32[2,144,144]{2,1,0:T(8,128)}, f32[2,144,768]{2,1,0:T(8,128)}, f32[2,384,144]{2,1,...) custom-call(bf16[128,2,16,128]{3,2,1,0:T(8,128)(2,1)} %copy-done), custom_call_target="tpu_custom_call" | custom-call | tf_op jit(solution)/shard_map/pallas_call | solution.py:618
  235.6 1.6 copy.30
  237.2 2.1 copy.31
  (126 shorter events, 38.7 us)
Async XLA Ops:
  2.6 16.9 %all-to-all-start = ((f32[32,2,128]{2,1,0:T(2,128)}), f32[32,2,128]{2,1,0:T(2,128)S(1)}, u32[]{:S(2)}, u32[]{:S(2)}) async-start(f32[32,2,128]{2,1,0:T(2,128)} %broadcast_in_dim.6), calls=%async_computation | async-start | bytes 65536 | tf_op jit(solution)/shard_map/all_to_all | solution.py:657
  40.0 4.3 %collective-permute-start.2 = (bf16[144,128]{1,0:T(8,128)(2,1)}, bf16[144,128]{1,0:T(8,128)(2,1)S(1)}, u32[]{:S(2)}, u32[]{:S(2)}) collective-permute-start(bf16[144,128]{1,0:T(8,128)(2,1)} %get-tuple-element.54.refs_15_), channel_id=1, source_target_pairs={{0,6},{1,7},{2,4},{3,5},{4,2},{5,3},{6,0},{7,1},{8,14},{9,15},{10,... | collective-permute-start | bytes 110600 | tf_op jit(solution)/shard_map/ppermute | solution.py:629
  41.0 4.6 %collective-permute-start.1 = (bf16[144,128]{1,0:T(8,128)(2,1)}, bf16[144,128]{1,0:T(8,128)(2,1)S(1)}, u32[]{:S(2)}, u32[]{:S(2)}) collective-permute-start(bf16[144,128]{1,0:T(8,128)(2,1)} %get-tuple-element.54.refs_15_), channel_id=1, source_target_pairs={{0,4},{1,5},{2,6},{3,7},{4,0},{5,1},{6,2},{7,3},{8,12},{9,13},{10,... | collective-permute-start | bytes 110600 | tf_op jit(solution)/shard_map/ppermute | solution.py:629
  42.2 3.4 %collective-permute-start = (bf16[144,128]{1,0:T(8,128)(2,1)}, bf16[144,128]{1,0:T(8,128)(2,1)S(1)}, u32[]{:S(2)}, u32[]{:S(2)}) collective-permute-start(bf16[144,128]{1,0:T(8,128)(2,1)} %get-tuple-element.54.refs_15_), channel_id=1, source_target_pairs={{0,2},{1,3},{2,0},{3,1},{4,6},{5,7},{6,4},{7,5},{8,10},{9,11},{10,... | collective-permute-start | bytes 110600 | tf_op jit(solution)/shard_map/ppermute | solution.py:629
  46.4 13.2 %collective-permute-start.5 = (bf16[4,144,128]{2,1,0:T(8,128)(2,1)S(1)}, bf16[4,144,128]{2,1,0:T(8,128)(2,1)S(1)}, u32[]{:S(2)}, u32[]{:S(2)}) collective-permute-start(bf16[4,144,128]{2,1,0:T(8,128)(2,1)S(1)} %pad_maximum_fusion.2.refs_0_), channel_id=1, source_target_pairs={{0,24},{1,25},{2,26},{3,27},{4,28},{5,29},{6,30},{7,31},{8,16},{9,... | collective-permute-start | bytes 442376 | tf_op jit(solution)/shard_map/ppermute | solution.py:629
  48.0 11.7 %collective-permute-start.4 = (bf16[4,144,128]{2,1,0:T(8,128)(2,1)S(1)}, bf16[4,144,128]{2,1,0:T(8,128)(2,1)S(1)}, u32[]{:S(2)}, u32[]{:S(2)}) collective-permute-start(bf16[4,144,128]{2,1,0:T(8,128)(2,1)S(1)} %pad_maximum_fusion.2.refs_0_), channel_id=1, source_target_pairs={{0,16},{1,17},{2,18},{3,19},{4,20},{5,21},{6,22},{7,23},{8,24},{9,... | collective-permute-start | bytes 442376 | tf_op jit(solution)/shard_map/ppermute | solution.py:629
  48.6 11.6 %collective-permute-start.3 = (bf16[4,144,128]{2,1,0:T(8,128)(2,1)S(1)}, bf16[4,144,128]{2,1,0:T(8,128)(2,1)S(1)}, u32[]{:S(2)}, u32[]{:S(2)}) collective-permute-start(bf16[4,144,128]{2,1,0:T(8,128)(2,1)S(1)} %pad_maximum_fusion.2.refs_0_), channel_id=1, source_target_pairs={{0,8},{1,9},{2,10},{3,11},{4,12},{5,13},{6,14},{7,15},{8,0},{9,1},... | collective-permute-start | bytes 442376 | tf_op jit(solution)/shard_map/ppermute | solution.py:629
  49.9 5.7 %collective-permute-start.11 = (f32[64,144]{1,0:T(8,128)S(1)}, f32[64,144]{1,0:T(8,128)S(1)}, u32[]{:S(2)}, u32[]{:S(2)}) collective-permute-start(f32[64,144]{1,0:T(8,128)S(1)} %bitcast.24), channel_id=1, source_target_pairs={{0,1},{1,3},{2,5},{3,7},{4,9},{5,11},{6,13},{7,15},{8,17},{9,19},{... | collective-permute-start | bytes 110600 | tf_op jit(solution)/shard_map/ppermute | solution.py:659
  51.4 9.5 %collective-permute-start.10 = (f32[64,144]{1,0:T(8,128)S(1)}, f32[64,144]{1,0:T(8,128)S(1)}, u32[]{:S(2)}, u32[]{:S(2)}) collective-permute-start(f32[64,144]{1,0:T(8,128)S(1)} %bitcast.23), channel_id=1, source_target_pairs={{0,0},{1,2},{2,4},{3,6},{4,8},{5,10},{6,12},{7,14},{8,16},{9,18},{... | collective-permute-start | bytes 110600 | tf_op jit(solution)/shard_map/ppermute | solution.py:659
  55.6 5.9 %collective-permute-start.6 = (bf16[4,144,128]{2,1,0:T(8,128)(2,1)S(1)}, bf16[4,144,128]{2,1,0:T(8,128)(2,1)S(1)}, u32[]{:S(2)}, u32[]{:S(2)}) collective-permute-start(bf16[4,144,128]{2,1,0:T(8,128)(2,1)S(1)} %pad_maximum_fusion.2.refs_0_), channel_id=1, source_target_pairs={{0,1},{1,0},{2,3},{3,2},{4,5},{5,4},{6,7},{7,6},{8,9},{9,8},{10,11... | collective-permute-start | bytes 442376 | tf_op jit(solution)/shard_map/ppermute | solution.py:629
  79.0 4.8 %collective-permute-start.16 = (bf16[192,128]{1,0:T(8,128)(2,1)}, bf16[192,128]{1,0:T(8,128)(2,1)S(1)}, u32[]{:S(2)}, u32[]{:S(2)}) collective-permute-start(bf16[192,128]{1,0:T(8,128)(2,1)} %get-tuple-element.57), channel_id=1, source_target_pairs={{0,6},{1,7},{2,4},{3,5},{4,2},{5,3},{6,0},{7,1},{8,14},{9,15},{10,... | collective-permute-start | bytes 147464 | tf_op jit(solution)/shard_map/ppermute | solution.py:629
  80.3 4.7 %collective-permute-start.15 = (bf16[192,128]{1,0:T(8,128)(2,1)}, bf16[192,128]{1,0:T(8,128)(2,1)S(1)}, u32[]{:S(2)}, u32[]{:S(2)}) collective-permute-start(bf16[192,128]{1,0:T(8,128)(2,1)} %get-tuple-element.57), channel_id=1, source_target_pairs={{0,4},{1,5},{2,6},{3,7},{4,0},{5,1},{6,2},{7,3},{8,12},{9,13},{10,... | collective-permute-start | bytes 147464 | tf_op jit(solution)/shard_map/ppermute | solution.py:629
  86.9 7.6 %collective-permute-start.19 = (bf16[4,192,128]{2,1,0:T(8,128)(2,1)S(1)}, bf16[4,192,128]{2,1,0:T(8,128)(2,1)S(1)}, u32[]{:S(2)}, u32[]{:S(2)}) collective-permute-start(bf16[4,192,128]{2,1,0:T(8,128)(2,1)S(1)} %pad_maximum_fusion.refs_0_), channel_id=1, source_target_pairs={{0,24},{1,25},{2,26},{3,27},{4,28},{5,29},{6,30},{7,31},{8,16},{9,... | collective-permute-start | bytes 589832 | tf_op jit(solution)/shard_map/ppermute | solution.py:629
  89.2 9.6 %collective-permute-start.18 = (bf16[4,192,128]{2,1,0:T(8,128)(2,1)S(1)}, bf16[4,192,128]{2,1,0:T(8,128)(2,1)S(1)}, u32[]{:S(2)}, u32[]{:S(2)}) collective-permute-start(bf16[4,192,128]{2,1,0:T(8,128)(2,1)S(1)} %pad_maximum_fusion.refs_0_), channel_id=1, source_target_pairs={{0,16},{1,17},{2,18},{3,19},{4,20},{5,21},{6,22},{7,23},{8,24},{9,... | collective-permute-start | bytes 589832 | tf_op jit(solution)/shard_map/ppermute | solution.py:629
  89.3 11.4 %collective-permute-start.17 = (bf16[4,192,128]{2,1,0:T(8,128)(2,1)S(1)}, bf16[4,192,128]{2,1,0:T(8,128)(2,1)S(1)}, u32[]{:S(2)}, u32[]{:S(2)}) collective-permute-start(bf16[4,192,128]{2,1,0:T(8,128)(2,1)S(1)} %pad_maximum_fusion.refs_0_), channel_id=1, source_target_pairs={{0,8},{1,9},{2,10},{3,11},{4,12},{5,13},{6,14},{7,15},{8,0},{9,1},... | collective-permute-start | bytes 589832 | tf_op jit(solution)/shard_map/ppermute | solution.py:629
  90.2 20.2 %collective-permute-start.20 = (bf16[4,192,128]{2,1,0:T(8,128)(2,1)S(1)}, bf16[4,192,128]{2,1,0:T(8,128)(2,1)S(1)}, u32[]{:S(2)}, u32[]{:S(2)}) collective-permute-start(bf16[4,192,128]{2,1,0:T(8,128)(2,1)S(1)} %pad_maximum_fusion.refs_0_), channel_id=1, source_target_pairs={{0,1},{1,0},{2,3},{3,2},{4,5},{5,4},{6,7},{7,6},{8,9},{9,8},{10,11... | collective-permute-start | bytes 589832 | tf_op jit(solution)/shard_map/ppermute | solution.py:629
  94.5 15.9 %collective-permute-start.23 = (bf16[4,192,128]{2,1,0:T(8,128)(2,1)S(1)}, bf16[4,192,128]{2,1,0:T(8,128)(2,1)S(1)}, u32[]{:S(2)}, u32[]{:S(2)}) collective-permute-start(bf16[4,192,128]{2,1,0:T(8,128)(2,1)S(1)} %collective-permute-done.19.refs_3_), channel_id=1, source_target_pairs={{0,1},{1,0},{2,3},{3,2},{4,5},{5,4},{6,7},{7,6},{8,9},{9,8},{10,11... | collective-permute-start | bytes 589832 | tf_op jit(solution)/shard_map/ppermute | solution.py:629
  98.8 11.6 %collective-permute-start.22 = (bf16[4,192,128]{2,1,0:T(8,128)(2,1)S(1)}, bf16[4,192,128]{2,1,0:T(8,128)(2,1)S(1)}, u32[]{:S(2)}, u32[]{:S(2)}) collective-permute-start(bf16[4,192,128]{2,1,0:T(8,128)(2,1)S(1)} %collective-permute-done.18.refs_2_), channel_id=1, source_target_pairs={{0,1},{1,0},{2,3},{3,2},{4,5},{5,4},{6,7},{7,6},{8,9},{9,8},{10,11... | collective-permute-start | bytes 589832 | tf_op jit(solution)/shard_map/ppermute | solution.py:629
  100.7 9.7 %collective-permute-start.21 = (bf16[4,192,128]{2,1,0:T(8,128)(2,1)S(1)}, bf16[4,192,128]{2,1,0:T(8,128)(2,1)S(1)}, u32[]{:S(2)}, u32[]{:S(2)}) collective-permute-start(bf16[4,192,128]{2,1,0:T(8,128)(2,1)S(1)} %collective-permute-done.17.refs_1_), channel_id=1, source_target_pairs={{0,1},{1,0},{2,3},{3,2},{4,5},{5,4},{6,7},{7,6},{8,9},{9,8},{10,11... | collective-permute-start | bytes 589832 | tf_op jit(solution)/shard_map/ppermute | solution.py:629
  124.3 4.4 %collective-permute-start.26 = (bf16[192,128]{1,0:T(8,128)(2,1)}, bf16[192,128]{1,0:T(8,128)(2,1)S(1)}, u32[]{:S(2)}, u32[]{:S(2)}) collective-permute-start(bf16[192,128]{1,0:T(8,128)(2,1)} %get-tuple-element.73), channel_id=1, source_target_pairs={{0,6},{1,7},{2,4},{3,5},{4,2},{5,3},{6,0},{7,1},{8,14},{9,15},{10,... | collective-permute-start | bytes 147464 | tf_op jit(solution)/shard_map/ppermute | solution.py:629
  126.3 4.7 %collective-permute-start.25 = (bf16[192,128]{1,0:T(8,128)(2,1)}, bf16[192,128]{1,0:T(8,128)(2,1)S(1)}, u32[]{:S(2)}, u32[]{:S(2)}) collective-permute-start(bf16[192,128]{1,0:T(8,128)(2,1)} %get-tuple-element.73), channel_id=1, source_target_pairs={{0,4},{1,5},{2,6},{3,7},{4,0},{5,1},{6,2},{7,3},{8,12},{9,13},{10,... | collective-permute-start | bytes 147464 | tf_op jit(solution)/shard_map/ppermute | solution.py:629
  127.4 3.6 %collective-permute-start.24 = (bf16[192,128]{1,0:T(8,128)(2,1)}, bf16[192,128]{1,0:T(8,128)(2,1)S(1)}, u32[]{:S(2)}, u32[]{:S(2)}) collective-permute-start(bf16[192,128]{1,0:T(8,128)(2,1)} %get-tuple-element.73), channel_id=1, source_target_pairs={{0,2},{1,3},{2,0},{3,1},{4,6},{5,7},{6,4},{7,5},{8,10},{9,11},{10,... | collective-permute-start | bytes 147464 | tf_op jit(solution)/shard_map/ppermute | solution.py:629
  131.9 9.8 %collective-permute-start.29 = (bf16[4,192,128]{2,1,0:T(8,128)(2,1)S(1)}, bf16[4,192,128]{2,1,0:T(8,128)(2,1)S(1)}, u32[]{:S(2)}, u32[]{:S(2)}) collective-permute-start(bf16[4,192,128]{2,1,0:T(8,128)(2,1)S(1)} %pad_maximum_fusion.1.refs_0_), channel_id=1, source_target_pairs={{0,24},{1,25},{2,26},{3,27},{4,28},{5,29},{6,30},{7,31},{8,16},{9,... | collective-permute-start | bytes 589832 | tf_op jit(solution)/shard_map/ppermute | solution.py:629
  134.2 9.9 %collective-permute-start.28 = (bf16[4,192,128]{2,1,0:T(8,128)(2,1)S(1)}, bf16[4,192,128]{2,1,0:T(8,128)(2,1)S(1)}, u32[]{:S(2)}, u32[]{:S(2)}) collective-permute-start(bf16[4,192,128]{2,1,0:T(8,128)(2,1)S(1)} %pad_maximum_fusion.1.refs_0_), channel_id=1, source_target_pairs={{0,16},{1,17},{2,18},{3,19},{4,20},{5,21},{6,22},{7,23},{8,24},{9,... | collective-permute-start | bytes 589832 | tf_op jit(solution)/shard_map/ppermute | solution.py:629
  134.2 11.0 %collective-permute-start.27 = (bf16[4,192,128]{2,1,0:T(8,128)(2,1)S(1)}, bf16[4,192,128]{2,1,0:T(8,128)(2,1)S(1)}, u32[]{:S(2)}, u32[]{:S(2)}) collective-permute-start(bf16[4,192,128]{2,1,0:T(8,128)(2,1)S(1)} %pad_maximum_fusion.1.refs_0_), channel_id=1, source_target_pairs={{0,8},{1,9},{2,10},{3,11},{4,12},{5,13},{6,14},{7,15},{8,0},{9,1},... | collective-permute-start | bytes 589832 | tf_op jit(solution)/shard_map/ppermute | solution.py:629
  135.2 19.7 %collective-permute-start.30 = (bf16[4,192,128]{2,1,0:T(8,128)(2,1)S(1)}, bf16[4,192,128]{2,1,0:T(8,128)(2,1)S(1)}, u32[]{:S(2)}, u32[]{:S(2)}) collective-permute-start(bf16[4,192,128]{2,1,0:T(8,128)(2,1)S(1)} %pad_maximum_fusion.1.refs_0_), channel_id=1, source_target_pairs={{0,1},{1,0},{2,3},{3,2},{4,5},{5,4},{6,7},{7,6},{8,9},{9,8},{10,11... | collective-permute-start | bytes 589832 | tf_op jit(solution)/shard_map/ppermute | solution.py:629
  141.7 13.2 %collective-permute-start.33 = (bf16[4,192,128]{2,1,0:T(8,128)(2,1)S(1)}, bf16[4,192,128]{2,1,0:T(8,128)(2,1)S(1)}, u32[]{:S(2)}, u32[]{:S(2)}) collective-permute-start(bf16[4,192,128]{2,1,0:T(8,128)(2,1)S(1)} %collective-permute-done.29.refs_3_), channel_id=1, source_target_pairs={{0,1},{1,0},{2,3},{3,2},{4,5},{5,4},{6,7},{7,6},{8,9},{9,8},{10,11... | collective-permute-start | bytes 589832 | tf_op jit(solution)/shard_map/ppermute | solution.py:629
  144.1 10.9 %collective-permute-start.32 = (bf16[4,192,128]{2,1,0:T(8,128)(2,1)S(1)}, bf16[4,192,128]{2,1,0:T(8,128)(2,1)S(1)}, u32[]{:S(2)}, u32[]{:S(2)}) collective-permute-start(bf16[4,192,128]{2,1,0:T(8,128)(2,1)S(1)} %collective-permute-done.28.refs_2_), channel_id=1, source_target_pairs={{0,1},{1,0},{2,3},{3,2},{4,5},{5,4},{6,7},{7,6},{8,9},{9,8},{10,11... | collective-permute-start | bytes 589832 | tf_op jit(solution)/shard_map/ppermute | solution.py:629
  145.1 9.8 %collective-permute-start.31 = (bf16[4,192,128]{2,1,0:T(8,128)(2,1)S(1)}, bf16[4,192,128]{2,1,0:T(8,128)(2,1)S(1)}, u32[]{:S(2)}, u32[]{:S(2)}) collective-permute-start(bf16[4,192,128]{2,1,0:T(8,128)(2,1)S(1)} %collective-permute-done.27.refs_1_), channel_id=1, source_target_pairs={{0,1},{1,0},{2,3},{3,2},{4,5},{5,4},{6,7},{7,6},{8,9},{9,8},{10,11... | collective-permute-start | bytes 589832 | tf_op jit(solution)/shard_map/ppermute | solution.py:629
  205.3 23.8 %all-to-all-start.2 = ((bf16[128,2,16,128]{3,2,1,0:T(8,128)(2,1)}), bf16[128,2,16,128]{3,2,1,0:T(8,128)(2,1)S(1)}, u32[]{:S(2)}, u32[]{:S(2)}) async-start(bf16[128,2,16,128]{3,2,1,0:T(8,128)(2,1)} %broadcast_in_dim.8), calls=%async_computation.2 | async-start | bytes 2097152 | tf_op jit(solution)/shard_map/all_to_all | solution.py:716
  209.9 14.8 %collective-permute-start.12 = (f32[64,144]{1,0:T(8,128)S(1)}, f32[64,144]{1,0:T(8,128)S(1)}, u32[]{:S(2)}, u32[]{:S(2)}) collective-permute-start(f32[64,144]{1,0:T(8,128)S(1)} %get-tuple-element.108), channel_id=1, source_target_pairs={{0,0},{2,1},{4,2},{6,3},{8,4},{10,5},{12,6},{14,7},{16,8},{18,9},{... | collective-permute-start | bytes 110600 | tf_op jit(solution)/shard_map/ppermute | solution.py:690
  217.5 8.4 %collective-permute-start.13 = (f32[64,144]{1,0:T(8,128)S(1)}, f32[64,144]{1,0:T(8,128)S(1)}, u32[]{:S(2)}, u32[]{:S(2)}) collective-permute-start(f32[64,144]{1,0:T(8,128)S(1)} %get-tuple-element.109), channel_id=1, source_target_pairs={{1,0},{3,1},{5,2},{7,3},{9,4},{11,5},{13,6},{15,7},{17,8},{19,9},{... | collective-permute-start | bytes 110600 | tf_op jit(solution)/shard_map/ppermute | solution.py:690
  (32 other events, 212.8 us)
